TPU v7x, 32 devices: a whole 2x2x4 slice. The times are simulated.
32 devices in a mesh: dp: 2 (over y), seq: 4 (over x, core), tensor: 4 (over z).
Axes of the slice: x: 2, y: 2, z: 4, core: 2. Of those that a mesh axis runs over, the one named last changes fastest.
Arguments:
- inputs: bfloat16 [6, 2048, 768], P('dp', 'seq'), may hold values from -6 to 6
- lengths: int32 [6], P('dp'), may hold values from 512 to 2048, as said below
- gain_attn: bfloat16 [768], P('dp'), may hold values from 0.5 to 1.5
- w_query: bfloat16 [768, 768], P('dp', 'tensor'), may hold values from -0.109375 to 0.109375
- w_key: bfloat16 [768, 768], P('dp', 'tensor'), may hold values from -0.109375 to 0.109375
- w_value: bfloat16 [768, 768], P('dp', 'tensor'), may hold values from -0.21875 to 0.21875
- w_out: bfloat16 [768, 768], P('tensor', 'dp'), may hold values from -1.75 to 1.75
- bias_table: bfloat16 [32, 12], P('dp', 'tensor'), may hold values from -4 to 4
- gain_ffn: bfloat16 [768], P('dp'), may hold values from 0.5 to 1.5
- w_in: bfloat16 [768, 3072], P('dp', 'tensor'), may hold values from -0.21875 to 0.21875
- w_down: bfloat16 [3072, 768], P('tensor', 'dp'), may hold values from -0.15625 to 0.15625
- cotangent: bfloat16 [6, 2048, 768], P('dp', 'seq'), may hold values from -6 to 6
Outputs:
- outputs: bfloat16 [6, 2048, 768], P('dp', 'seq')
- grad_inputs: bfloat16 [6, 2048, 768], P('dp', 'seq')
- grad_gain_attn: float32 [768], P('dp')
- grad_query: float32 [768, 768], P('dp', 'tensor')
- grad_key: float32 [768, 768], P('dp', 'tensor')
- grad_value: float32 [768, 768], P('dp', 'tensor')
- grad_out: float32 [768, 768], P('tensor', 'dp')
- grad_table: float32 [32, 12], P('dp', 'tensor')
- grad_gain_ffn: float32 [768], P('dp')
- grad_in: float32 [768, 3072], P('dp', 'tensor')
- grad_down: float32 [3072, 768], P('tensor', 'dp')
Inputs may be any that keep to these rules, and one draw needn't show every extreme that they name: `lengths`: real tokens of each sequence, counted from its first slot; in every draw some sequence fills all 2048 slots.
All inputs are finite; a program needn't handle non-finite values.
Results may differ from a plain program's by a relative error of at most 0.019.
Values may be sent and summed in bfloat16 or wider, within the bound.
No kernel may reach another device: no remote copies, remote signals or barrier semaphores. Data moves between devices by JAX's collectives and lax.ppermute only.
A program may use at most 256 MiB of HBM per device.

v0:
```python
import jax
import jax.numpy as jnp
from jax import lax
from jax.sharding import PartitionSpec as P

HEAD = 64
BUCKETS = 32


EPSILON = 1e-06
LIMITS = (12, 16, 23, 32, 46, 64, 91)
HIGHEST = lax.Precision.HIGHEST


def bucket_of(relative):
    sign_part = jnp.where(relative > 0, 16, 0).astype(jnp.int32)
    distance = jnp.abs(relative)
    far_part = jnp.full(distance.shape, 8, jnp.int32)
    for limit in LIMITS:
        far_part = far_part + (distance >= limit).astype(jnp.int32)
    return sign_part + jnp.where(distance < 8, distance, far_part)


def smooth_act(values):
    return jax.nn.gelu(values, approximate=True)


def smooth_back(hidden, grad_active):
    _, pull = jax.vjp(smooth_act, hidden)
    return pull(grad_active)[0]


def norm_rows(values, gain):
    scale = lax.rsqrt(jnp.mean(values * values, axis=-1, keepdims=True) + EPSILON)
    return (values * scale * gain, scale)


def norm_back(grad_norm, values, scale, gain):
    unit_rows = values * scale
    along_rows = grad_norm * gain
    grad_values = scale * (
        along_rows - unit_rows * jnp.mean(along_rows * unit_rows, axis=-1, keepdims=True)
    )
    return (grad_values, jnp.sum(grad_norm * unit_rows, axis=0))


def toeplitz(relvec, first_row, row_count, col_count):
    half_width = relvec.shape[1] // 2
    offset = half_width - row_count - first_row
    window = lax.dynamic_slice_in_dim(relvec, offset, col_count + row_count, 1)
    head_count = relvec.shape[0]
    tiled = jnp.broadcast_to(window[:, None, :], (head_count, row_count, col_count + row_count))
    tiled = tiled.reshape(head_count, row_count * (col_count + row_count))
    tiled = tiled[:, : row_count * (col_count + row_count - 1)].reshape(
        head_count, row_count, col_count + row_count - 1
    )
    return tiled[:, :, row_count - 1 : row_count - 1 + col_count]


def body(
    inputs,
    lengths,
    gain_attn,
    w_query,
    w_key,
    w_value,
    w_out,
    bias_table,
    gain_ffn,
    w_in,
    w_down,
    cotangent,
):
    slots_here, rows_here, feature_count = inputs.shape
    full_len = rows_here * lax.axis_size("seq")
    first_row = lax.axis_index("seq") * rows_here
    row_pos = first_row + jnp.arange(rows_here, dtype=jnp.int32)
    key_pos = jnp.arange(full_len, dtype=jnp.int32)
    relative = jnp.arange(2 * full_len, dtype=jnp.int32) - (full_len - 1)
    selector = (
        bucket_of(relative)[:, None] == jnp.arange(BUCKETS, dtype=jnp.int32)[None, :]
    ).astype(jnp.float32)
    totals = None
    out_rows = []
    grad_rows = []
    for member in range(slots_here):
        whole = (
            lax.all_gather(gain_attn, "dp", axis=0, tiled=True),
            lax.all_gather(w_query, "dp", axis=0, tiled=True),
            lax.all_gather(w_key, "dp", axis=0, tiled=True),
            lax.all_gather(w_value, "dp", axis=0, tiled=True),
            lax.all_gather(w_out, "dp", axis=1, tiled=True),
            lax.all_gather(bias_table, "dp", axis=0, tiled=True),
            lax.all_gather(gain_ffn, "dp", axis=0, tiled=True),
            lax.all_gather(w_in, "dp", axis=0, tiled=True),
            lax.all_gather(w_down, "dp", axis=1, tiled=True),
        )
        (
            gain_one,
            query_full,
            key_full,
            value_full,
            out_full,
            table_full,
            gain_two,
            in_full,
            down_full,
        ) = whole
        gain_one = gain_one.astype(jnp.float32)
        gain_two = gain_two.astype(jnp.float32)
        head_count = query_full.shape[1] // HEAD
        length = lengths[member]
        key_live = key_pos < length
        resid_in = inputs[member].astype(jnp.float32)
        normed, scale_one = norm_rows(resid_in, gain_one)
        normed_low = normed.astype(jnp.bfloat16)
        query = jnp.dot(normed_low, query_full, preferred_element_type=jnp.float32).astype(
            jnp.bfloat16
        )
        key_rows = jnp.dot(normed_low, key_full, preferred_element_type=jnp.float32).astype(
            jnp.bfloat16
        )
        value_rows = jnp.dot(normed_low, value_full, preferred_element_type=jnp.float32).astype(
            jnp.bfloat16
        )
        keys_all, values_all = (
            lax.all_gather(key_rows, "seq", axis=0, tiled=True),
            lax.all_gather(value_rows, "seq", axis=0, tiled=True),
        )
        query_heads = query.reshape(rows_here, head_count, HEAD)
        key_heads = keys_all.reshape(full_len, head_count, HEAD)
        value_heads = values_all.reshape(full_len, head_count, HEAD)
        relvec = jnp.dot(selector, table_full.astype(jnp.float32), precision=HIGHEST).T
        position_bias = toeplitz(relvec, first_row, rows_here, full_len)
        scores = (
            jnp.einsum("qhe,khe->hqk", query_heads, key_heads, preferred_element_type=jnp.float32)
            + position_bias
        )
        scores = jnp.where(key_live[None, None, :], scores, -1e30)
        top_score = jnp.max(scores, axis=-1, keepdims=True)
        log_total = top_score + jnp.log(
            jnp.sum(jnp.exp(scores - top_score), axis=-1, keepdims=True)
        )
        probs = jnp.exp(scores - log_total)
        probs_low = probs.astype(jnp.bfloat16)
        mixed = jnp.einsum(
            "hqk,khe->qhe", probs_low, value_heads, preferred_element_type=jnp.float32
        )
        mixed = mixed.reshape(rows_here, head_count * HEAD).astype(jnp.bfloat16)
        attn_part = jnp.dot(mixed, out_full, preferred_element_type=jnp.float32)
        live_rows = (row_pos < length).astype(jnp.float32)
        grad_float = cotangent[member].astype(jnp.float32) * live_rows[:, None]
        grad_low = grad_float.astype(jnp.bfloat16)
        resid_mid = resid_in + lax.psum(attn_part, "tensor")
        normed_two, scale_two = norm_rows(resid_mid, gain_two)
        normed_two_low = normed_two.astype(jnp.bfloat16)
        hidden = jnp.dot(normed_two_low, in_full, preferred_element_type=jnp.float32)
        active = smooth_act(hidden).astype(jnp.bfloat16)
        ffn_total = lax.psum(
            jnp.dot(active, down_full, preferred_element_type=jnp.float32).astype(jnp.bfloat16),
            "tensor",
        ).astype(jnp.float32)
        out_rows.append((resid_mid + ffn_total).astype(jnp.bfloat16))
        d_down = jnp.einsum("cf,cd->fd", active, grad_low, preferred_element_type=jnp.float32)
        d_active = jnp.einsum("cd,fd->cf", grad_low, down_full, preferred_element_type=jnp.float32)
        d_hidden = smooth_back(hidden, d_active).astype(jnp.bfloat16)
        d_in = jnp.einsum("cd,cf->df", normed_two_low, d_hidden, preferred_element_type=jnp.float32)
        d_normed_two = lax.psum(
            jnp.einsum("cf,df->cd", d_hidden, in_full, preferred_element_type=jnp.float32), "tensor"
        )
        d_norm_two, d_gain_two = norm_back(d_normed_two, resid_mid, scale_two, gain_two)
        d_resid = grad_float + d_norm_two
        d_resid_low = d_resid.astype(jnp.bfloat16)
        d_out = jnp.einsum("cj,cd->jd", mixed, d_resid_low, preferred_element_type=jnp.float32)
        d_mixed = jnp.einsum(
            "cd,jd->cj", d_resid_low, out_full, preferred_element_type=jnp.float32
        ).astype(jnp.bfloat16)
        d_mixed = d_mixed.reshape(rows_here, head_count, HEAD)
        d_probs = jnp.einsum(
            "qhe,khe->hqk", d_mixed, value_heads, preferred_element_type=jnp.float32
        )
        d_scores = probs * (d_probs - jnp.sum(probs * d_probs, axis=-1, keepdims=True))
        d_scores_low = d_scores.astype(jnp.bfloat16)
        d_query = jnp.einsum(
            "hqk,khe->qhe", d_scores_low, key_heads, preferred_element_type=jnp.float32
        )
        d_query = d_query.reshape(rows_here, head_count * HEAD).astype(jnp.bfloat16)
        part_keys = jnp.einsum(
            "hqk,qhe->khe", d_scores_low, query_heads, preferred_element_type=jnp.float32
        ).reshape(full_len, head_count * HEAD)
        part_values = jnp.einsum(
            "hqk,qhe->khe", probs_low, d_mixed, preferred_element_type=jnp.float32
        ).reshape(full_len, head_count * HEAD)
        d_keys, d_values = (
            lax.psum_scatter(part_keys, "seq", scatter_dimension=0, tiled=True),
            lax.psum_scatter(part_values, "seq", scatter_dimension=0, tiled=True),
        )
        d_keys = d_keys.astype(jnp.bfloat16)
        d_values = d_values.astype(jnp.bfloat16)
        _, pull_bias = jax.vjp(
            lambda vector: toeplitz(vector, first_row, rows_here, full_len), relvec
        )
        (d_relvec,) = pull_bias(d_scores_low.astype(jnp.float32))
        d_table = jnp.einsum("rb,hr->bh", selector, d_relvec, precision=HIGHEST)
        d_wquery = jnp.einsum("cd,cj->dj", normed_low, d_query, preferred_element_type=jnp.float32)
        d_wkey = jnp.einsum("cd,cj->dj", normed_low, d_keys, preferred_element_type=jnp.float32)
        d_wvalue = jnp.einsum("cd,cj->dj", normed_low, d_values, preferred_element_type=jnp.float32)
        d_normed_part = jnp.einsum(
            "cj,dj->cd", d_query, query_full, preferred_element_type=jnp.float32
        )
        d_normed_part = d_normed_part + jnp.einsum(
            "cj,dj->cd", d_keys, key_full, preferred_element_type=jnp.float32
        )
        d_normed_part = d_normed_part + jnp.einsum(
            "cj,dj->cd", d_values, value_full, preferred_element_type=jnp.float32
        )
        d_normed_one = lax.psum(d_normed_part, "tensor")
        d_norm_one, d_gain_one = norm_back(d_normed_one, resid_in, scale_one, gain_one)
        grad_rows.append((d_resid + d_norm_one).astype(jnp.bfloat16))
        step_grads = (
            d_gain_one,
            d_wquery,
            d_wkey,
            d_wvalue,
            d_out,
            d_table,
            d_gain_two,
            d_in,
            d_down,
        )
        step_grads = tuple(step_grads)
        if member == 0:
            totals = step_grads
        else:
            totals = tuple((total + extra for total, extra in zip(totals, step_grads)))
    totals = (
        lax.psum_scatter(totals[0], "dp", scatter_dimension=0, tiled=True),
        lax.psum_scatter(totals[1], "dp", scatter_dimension=0, tiled=True),
        lax.psum_scatter(totals[2], "dp", scatter_dimension=0, tiled=True),
        lax.psum_scatter(totals[3], "dp", scatter_dimension=0, tiled=True),
        lax.psum_scatter(totals[4], "dp", scatter_dimension=1, tiled=True),
        lax.psum_scatter(totals[5], "dp", scatter_dimension=0, tiled=True),
        lax.psum_scatter(totals[6], "dp", scatter_dimension=0, tiled=True),
        lax.psum_scatter(totals[7], "dp", scatter_dimension=0, tiled=True),
        lax.psum_scatter(totals[8], "dp", scatter_dimension=1, tiled=True),
    )
    totals = lax.psum(totals, "seq")
    gain_first = totals[0]
    gain_second = totals[6]
    return (
        jnp.stack(out_rows),
        jnp.stack(grad_rows),
        gain_first,
        totals[1],
        totals[2],
        totals[3],
        totals[4],
        totals[5],
        gain_second,
        totals[7],
        totals[8],
    )


def solution(mesh):
    in_specs = (
        P("dp", "seq", None),
        P("dp"),
        P("dp"),
        P("dp", "tensor"),
        P("dp", "tensor"),
        P("dp", "tensor"),
        P("tensor", "dp"),
        P("dp", "tensor"),
        P("dp"),
        P("dp", "tensor"),
        P("tensor", "dp"),
        P("dp", "seq", None),
    )
    out_specs = (
        P("dp", "seq", None),
        P("dp", "seq", None),
        P("dp"),
        P("dp", "tensor"),
        P("dp", "tensor"),
        P("dp", "tensor"),
        P("tensor", "dp"),
        P("dp", "tensor"),
        P("dp"),
        P("dp", "tensor"),
        P("tensor", "dp"),
    )
    return jax.shard_map(body, mesh=mesh, in_specs=in_specs, out_specs=out_specs, check_vma=False)
```

profile of v0, /device:TPU:0, one launch (start us, length us, event | category | flops | bytes accessed | tf_op | source)
XLA Modules:
  0.0 1368.4 jit_solution(17931228019921551223)
XLA Ops:
  8.8 5.2 all-gather
  16.5 5.8 all_gather.67
  22.3 5.8 all_gather.66
  31.5 5.8 all_gather.31
  43.2 9.1 all_gather.68
  58.8 33.0 %copy.28 = f32[1,3,512,2560]{3,1,2,0:T(4,128)S(1)} copy(f32[1,3,512,2560]{3,2,1,0:T(8,128)S(1)} %broadcast_bitcast_fusion) | data formatting | bytes 31457280
  91.8 9.4 slice.48
  101.2 44.9 %reshape.408 = f32[3930624]{0:T(1024)} reshape(f32[3,1310208]{1,0:T(4,128)} %slice.48) | data formatting | bytes 31444992
  146.1 23.1 %reshape.354 = f32[3,512,2559]{2,1,0:T(8,128)} reshape(f32[3930624]{0:T(1024)} %reshape.408) | data formatting | bytes 31444992 | tf_op jit(solution)/shard_map/reshape | solution.py:54
  170.6 7.1 fusion.213
  182.2 7.7 all_gather.32
  189.9 6.8 all_gather.70
  196.7 8.7 all_gather.75
  206.1 6.9 fusion.212
  215.0 8.7 all_gather.74
  223.7 7.0 fusion.93
  236.3 8.7 all_gather.77
  245.5 7.1 fusion.211
  254.6 8.7 all_gather.76
  275.6 165.8 %all-reduce.25.cloned.1.call-done = (f32[512,768]{1,0:T(8,128)}, f32[512,768]{1,0:T(8,128)}, f32[512,768]{1,0:T(8,128)}) async-done(((f32[512,768]{1,0:T(8,128)}, f32[512,768]{1,0:T(8,128)}, f32[512,768]{1,0:T(8,128)}), (f32[512,768]{1,0:T(8,128)}, f32[512,768]{1,0:T(8,128)}, f32[512,768]{1,0:T(8,128)})) %all-reduce.25.cloned.1.call-update) | async-done | bytes 4718608 | tf_op jit(solution)/shard_map/psum | solution.py:154
  441.4 4.7 multiply_reduce_fusion.11
  476.2 79.6 %all-reduce.29.cloned.1.call-done = (bf16[512,768]{1,0:T(8,128)(2,1)}, bf16[512,768]{1,0:T(8,128)(2,1)}, bf16[512,768]{1,0:T(8,128)(2,1)}) async-done(((bf16[512,768]{1,0:T(8,128)(2,1)}, bf16[512,768]{1,0:T(8,128)(2,1)}, bf16[512,768]{1,0:T(8,128)(2,1)}), (bf16[512,768]{1,0:T(8,128)(2,1)}, bf16[512,768]{1,0:T(8,128)(2,1)}, bf16[512,768]{1,0:T(8,128)(2,1)})) %all-reduce.29.cloned.1.call-update) | async-done | bytes 2359312 | tf_op jit(solution)/shard_map/psum | solution.py:159
  555.9 174.8 %all-reduce.23.cloned.1.call-done = (f32[512,768]{1,0:T(8,128)}, f32[512,768]{1,0:T(8,128)}, f32[512,768]{1,0:T(8,128)}) async-done(((f32[512,768]{1,0:T(8,128)}, f32[512,768]{1,0:T(8,128)}, f32[512,768]{1,0:T(8,128)}), (f32[512,768]{1,0:T(8,128)}, f32[512,768]{1,0:T(8,128)}, f32[512,768]{1,0:T(8,128)})) %all-reduce.23.cloned.1.call-update) | async-done | bytes 4718608 | tf_op jit(solution)/shard_map/psum | solution.py:168
  730.7 5.9 multiply_reduce_fusion.5
  736.7 5.1 fusion.91
  751.7 8.4 fusion.28
  764.4 10.4 multiply_reduce_fusion.2
  775.5 6.3 multiply_convert_fusion.2
  784.5 7.1 pad.24
  791.6 21.2 %reshape.410 = bf16[3930624]{0:T(1024)(128)(2,1)} reshape(bf16[3,512,2559]{2,1,0:T(8,128)(2,1)} %pad.24) | data formatting | bytes 15722496
  812.8 11.5 reshape.370
  824.8 7.9 fusion.24
  832.7 14.7 %pad_convert_fusion.2 = f32[3,1310720]{1,0:T(4,128)} fusion(bf16[3,1310208]{1,0:T(4,128)(2,1)} %reshape.370), kind=kLoop, calls=%fused_computation.20 | loop fusion | flops 3932160 | bytes 23589888 | tf_op jit(solution)/shard_map/transpose(jvp())/reshape | solution.py:53
  847.5 9.2 multiply_reduce_fusion.1
  856.7 6.3 multiply_convert_fusion.1
  865.7 7.1 pad.26
  872.8 20.7 %reshape.412 = bf16[3930624]{0:T(1024)(128)(2,1)} reshape(bf16[3,512,2559]{2,1,0:T(8,128)(2,1)} %pad.26) | data formatting | bytes 15722496
  893.5 11.4 reshape.373
  905.0 5.2 fusion.219
  910.2 14.8 %pad_convert_fusion.1 = f32[3,1310720]{1,0:T(4,128)} fusion(bf16[3,1310208]{1,0:T(4,128)(2,1)} %reshape.373), kind=kLoop, calls=%fused_computation.19 | loop fusion | flops 3932160 | bytes 23589888 | tf_op jit(solution)/shard_map/transpose(jvp())/reshape | solution.py:53
  925.0 9.2 multiply_reduce_fusion
  934.3 6.3 multiply_convert_fusion
  943.3 7.0 pad.28
  950.3 20.7 %reshape.414 = bf16[3930624]{0:T(1024)(128)(2,1)} reshape(bf16[3,512,2559]{2,1,0:T(8,128)(2,1)} %pad.28) | data formatting | bytes 15722496
  971.1 11.4 reshape.376
  982.5 5.2 fusion.222
  987.7 12.2 pad_convert_fusion
  1000.0 5.2 fusion.225
  1005.2 11.2 bitcast_reduce_fusion.2
  1016.8 11.4 bitcast_reduce_fusion.1
  1028.6 11.6 bitcast_reduce_fusion
  1041.4 5.2 add_add_fusion
  1058.6 4.9 convolution_convert_fusion.5
  1063.6 5.7 convolution_convert_fusion.4
  1071.2 4.8 convolution_convert_fusion.3
  1110.0 21.6 %reduce-scatter.36.cloned.1.call-done = f32[384,768]{1,0:T(8,128)} async-done(((f32[768,768]{1,0:T(8,128)}), f32[384,768]{1,0:T(8,128)}) %reduce-scatter.36.cloned.1.call-update) | async-done | bytes 1179664 | tf_op jit(solution)/shard_map/reduce_scatter | solution.py:244
  1131.6 17.5 %reduce-scatter.34.cloned.1.call-done = f32[192,384]{1,0:T(8,128)} async-done(((f32[192,768]{1,0:T(8,128)}), f32[192,384]{1,0:T(8,128)}) %reduce-scatter.34.cloned.1.call-update) | async-done | bytes 294928 | tf_op jit(solution)/shard_map/reduce_scatter | solution.py:241
  1149.1 17.5 %reduce-scatter.28.cloned.1.call-done = f32[384,192]{0,1:T(8,128)} async-done(((f32[768,192]{0,1:T(8,128)}), f32[384,192]{0,1:T(8,128)}) %reduce-scatter.28.cloned.1.call-update) | async-done | bytes 294928 | tf_op jit(solution)/shard_map/reduce_scatter | solution.py:238
  1166.6 17.5 %reduce-scatter.32.cloned.1.call-done = f32[384,192]{0,1:T(8,128)} async-done(((f32[768,192]{0,1:T(8,128)}), f32[384,192]{0,1:T(8,128)}) %reduce-scatter.32.cloned.1.call-update) | async-done | bytes 294928 | tf_op jit(solution)/shard_map/reduce_scatter | solution.py:240
  1184.0 17.6 %reduce-scatter.30.cloned.1.call-done = f32[384,192]{0,1:T(8,128)} async-done(((f32[768,192]{0,1:T(8,128)}), f32[384,192]{0,1:T(8,128)}) %reduce-scatter.30.cloned.1.call-update) | async-done | bytes 294928 | tf_op jit(solution)/shard_map/reduce_scatter | solution.py:239
  1201.6 73.5 %all-reduce.21.cloned.1.call-done = (f32[512,768]{1,0:T(8,128)}, f32[512,768]{1,0:T(8,128)}, f32[512,768]{1,0:T(8,128)}) async-done(((f32[512,768]{1,0:T(8,128)}, f32[512,768]{1,0:T(8,128)}, f32[512,768]{1,0:T(8,128)}), (f32[512,768]{1,0:T(8,128)}, f32[512,768]{1,0:T(8,128)}, f32[512,768]{1,0:T(8,128)})) %all-reduce.21.cloned.1.call-update) | async-done | bytes 4718608 | tf_op jit(solution)/shard_map/psum | solution.py:217
  1278.3 5.0 all-reduce.13
  1283.4 7.0 all-reduce.11
  1296.6 56.2 %all-reduce.27.cloned.1.call-done = (f32[384,192]{0,1:T(8,128)}, f32[384,192]{0,1:T(8,128)}, f32[384,192]{0,1:T(8,128)}, f32[192,384]{1,0:T(8,128)}, f32[384,768]{1,0:T(8,128)}, /*index=5*/f32[768,384]{1,0:T(8,128)}) async-done(((f32[384,192]{0,1:T(8,128)}, f32[384,192]{0,1:T(8,128)}, f32[384,192]{0,1:T(8,128)}, f32[192,384]{1,0:T(8,128)}, f32[384,768]{1,0:T(8,128)}, /*index=5*/f32[768,384]{1,0:T(8,128)}), ...) | async-done | bytes 3538960 | tf_op jit(solution)/shard_map/psum | solution.py:247
  (434 shorter events, 166.9 us)
Async XLA Ops:
  8.0 14.3 %copy-start.90 = (bf16[384,192]{0,1:T(8,128)(2,1)S(1)}, bf16[384,192]{0,1:T(8,128)(2,1)}, u32[]{:S(2)}) copy-start(bf16[384,192]{0,1:T(8,128)(2,1)} %param.15) | copy-start | bytes 442372
  8.0 433.4 %all-reduce.25.cloned.1.call-start = ((), (), s32[]{:S(2)}) async-start(), calls=%async_computation.30 | async-start | bytes 9437184 | tf_op jit(solution)/shard_map/psum | solution.py:154
  8.1 48.5 %copy-start.110 = (s32[4096]{0:T(1024)}, s32[4096]{0:T(1024)S(1)}, u32[]{:S(2)}) copy-start(s32[4096]{0:T(1024)S(1)} %fusion.171) | copy-start | bytes 49156
  14.1 27.9 %copy-start.82 = (f32[768]{0:T(1024)}, f32[768]{0:T(1024)S(1)}, u32[]{:S(2)}) copy-start(f32[768]{0:T(1024)S(1)} %reshape.397) | copy-start | bytes 9220
  14.1 14.0 %copy-start.6 = (bf16[3,512,768]{2,1,0:T(8,128)(2,1)S(1)}, bf16[3,512,768]{2,1,0:T(8,128)(2,1)}, u32[]{:S(2)}) copy-start(bf16[3,512,768]{2,1,0:T(8,128)(2,1)} %param.12) | copy-start | bytes 7077892
  16.4 20.9 %copy-start.105 = (f32[512]{0:T(512)}, f32[512]{0:T(512)S(1)}, u32[]{:S(2)}) copy-start(f32[512]{0:T(512)S(1)} %add_rsqrt_fusion.5) | copy-start | bytes 6148
  22.3 17.4 %copy-start.42 = (bf16[768,192]{0,1:T(8,128)(2,1)}, bf16[768,192]{0,1:T(8,128)(2,1)S(1)}, u32[]{:S(2)}) copy-start(bf16[768,192]{0,1:T(8,128)(2,1)S(1)} %all_gather.67) | copy-start | bytes 884740
  28.1 12.7 copy-start.44
  29.1 141.5 %copy-start.69 = (bf16[512,192]{0,1:T(8,128)(2,1)}, bf16[512,192]{0,1:T(8,128)(2,1)S(1)}, u32[]{:S(2)}) copy-start(bf16[512,192]{0,1:T(8,128)(2,1)S(1)} %convolution_convert_fusion.16) | copy-start | bytes 589828
  29.1 9.3 copy-start.99
  42.0 10.3 copy-start.113
  52.3 118.3 %copy-start.22 = (bf16[2048,192]{0,1:T(8,128)(2,1)}, bf16[2048,192]{0,1:T(8,128)(2,1)S(1)}, u32[]{:S(2)}) copy-start(bf16[2048,192]{0,1:T(8,128)(2,1)S(1)} %all_gather.68) | copy-start | bytes 2359300
  146.1 23.1 %copy-start.112 = (s32[3]{0:T(128)S(1)}, s32[3]{0:T(128)}, u32[]{:S(2)}) copy-start(s32[3]{0:T(128)} %param.13) | copy-start | bytes 40
  177.7 12.2 copy-start.92
  182.2 14.5 %copy-start.87 = (bf16[512,192]{0,1:T(8,128)(2,1)S(1)}, bf16[512,192]{0,1:T(8,128)(2,1)}, u32[]{:S(2)}) copy-start(bf16[512,192]{0,1:T(8,128)(2,1)} %convolution_convert_fusion.12) | copy-start | bytes 589828
  182.2 23.9 %copy-start.67 = (bf16[512,192]{0,1:T(8,128)(2,1)S(1)}, bf16[512,192]{0,1:T(8,128)(2,1)}, u32[]{:S(2)}) copy-start(bf16[512,192]{0,1:T(8,128)(2,1)} %convolution_convert_fusion.13) | copy-start | bytes 589828
  189.9 33.8 %copy-start.32 = (bf16[2048,192]{0,1:T(8,128)(2,1)}, bf16[2048,192]{0,1:T(8,128)(2,1)S(1)}, u32[]{:S(2)}) copy-start(bf16[2048,192]{0,1:T(8,128)(2,1)S(1)} %all_gather.32) | copy-start | bytes 2359300
  213.0 19.2 %copy-start.1 = (f32[3,512,2048]{2,1,0:T(8,128)}, f32[3,512,2048]{2,1,0:T(8,128)S(1)}, u32[]{:S(2)}) copy-start(f32[3,512,2048]{2,1,0:T(8,128)S(1)} %get-tuple-element.84) | copy-start | bytes 37748740
  234.7 18.0 %copy-start.52 = (bf16[3,64,512]{2,1,0:T(8,128)(2,1)}, bf16[3,64,512]{2,1,0:T(8,128)(2,1)S(1)}, u32[]{:S(2)}) copy-start(bf16[3,64,512]{2,1,0:T(8,128)(2,1)S(1)} %fusion.96) | copy-start | bytes 589828
  234.7 10.8 copy-start.65
  252.7 10.7 copy-start
  268.1 178.2 %all-gather.6.cloned.1.call-start = ((), (), s32[]{:S(2)}) async-start(), calls=%async_computation.13 | async-start | bytes 1769472 | tf_op jit(solution)/shard_map/all_gather | solution.py:95
  268.6 182.4 %all-gather.8.cloned.1.call-start = ((), (), s32[]{:S(2)}) async-start(), calls=%async_computation.14 | async-start | bytes 1769472 | tf_op jit(solution)/shard_map/all_gather | solution.py:96
  269.2 286.6 %all-reduce.29.cloned.1.call-start = ((), (), s32[]{:S(2)}) async-start(), calls=%async_computation.32 | async-start | bytes 4718592 | tf_op jit(solution)/shard_map/psum | solution.py:159
  271.2 465.4 %copy-start.103 = (f32[512]{0:T(512)}, f32[512]{0:T(512)S(1)}, u32[]{:S(2)}) copy-start(f32[512]{0:T(512)S(1)} %fusion.186) | copy-start | bytes 6148
  275.6 461.0 %copy-start.79 = (f32[768]{0:T(1024)}, f32[768]{0:T(1024)S(1)}, u32[]{:S(2)}) copy-start(f32[768]{0:T(1024)S(1)} %reshape.398) | copy-start | bytes 9220
  446.2 290.5 %copy-start.93 = (f32[512]{0:T(512)}, f32[512]{0:T(512)S(1)}, u32[]{:S(2)}) copy-start(f32[512]{0:T(512)S(1)} %add_rsqrt_fusion.4) | copy-start | bytes 6148
  446.2 290.5 %copy-start.95 = (f32[512]{0:T(512)}, f32[512]{0:T(512)S(1)}, u32[]{:S(2)}) copy-start(f32[512]{0:T(512)S(1)} %get-tuple-element.96) | copy-start | bytes 6148
  446.2 290.5 %copy-start.97 = (f32[512]{0:T(512)}, f32[512]{0:T(512)S(1)}, u32[]{:S(2)}) copy-start(f32[512]{0:T(512)S(1)} %get-tuple-element.95) | copy-start | bytes 6148
  460.4 270.3 %all-reduce.23.cloned.1.call-start = ((), (), s32[]{:S(2)}) async-start(), calls=%async_computation.29 | async-start | bytes 9437184 | tf_op jit(solution)/shard_map/psum | solution.py:168
  476.2 254.5 %copy-start.10 = (f32[512,768]{1,0:T(8,128)S(1)}, f32[512,768]{1,0:T(8,128)}, u32[]{:S(2)}) copy-start(f32[512,768]{1,0:T(8,128)} %get-tuple-element.54) | copy-start | bytes 4718596
  476.2 602.9 %reduce-scatter.18.cloned.1.call-start = ((), (), s32[]{:S(2)}) async-start(), calls=%async_computation.16 | async-start | bytes 1966080 | tf_op jit(solution)/shard_map/reduce_scatter | solution.py:196
  730.7 12.7 slice-start.6
  730.7 12.7 slice-start.7
  746.8 334.5 %reduce-scatter.22.cloned.1.call-start = ((), (), s32[]{:S(2)}) async-start(), calls=%async_computation.18 | async-start | bytes 1966080 | tf_op jit(solution)/shard_map/reduce_scatter | solution.py:196
  760.1 322.9 %reduce-scatter.26.cloned.1.call-start = ((), (), s32[]{:S(2)}) async-start(), calls=%async_computation.20 | async-start | bytes 1966080 | tf_op jit(solution)/shard_map/reduce_scatter | solution.py:196
  760.1 14.7 %slice-start.9 = ((s8[12582912]{0:T(1024)(128)(4,1)}), s8[4194304]{0:T(1024)(128)(4,1)S(1)}, s32[]{:S(2)}) async-start(s8[12582912]{0:T(1024)(128)(4,1)} %bitcast.329), calls=%async_computation.42 | async-start | bytes 8388608
  764.4 10.4 slice-start.10
  764.4 11.0 slice-start.11
  812.8 11.5 copy-start.17
  832.7 14.8 %copy-start.31 = (bf16[2048,192]{0,1:T(8,128)(2,1)S(1)}, bf16[2048,192]{0,1:T(8,128)(2,1)}, u32[]{:S(2)}) copy-start(bf16[2048,192]{0,1:T(8,128)(2,1)} %copy-done.30) | copy-start | bytes 2359300
  832.7 255.8 %reduce-scatter.16.cloned.1.call-start = ((), (), s32[]{:S(2)}) async-start(), calls=%async_computation.15 | async-start | bytes 1966080 | tf_op jit(solution)/shard_map/reduce_scatter | solution.py:195
  832.7 24.0 %slice-start.3 = ((s8[12582912]{0:T(1024)(128)(4,1)}), s8[4194304]{0:T(1024)(128)(4,1)S(1)}, s32[]{:S(2)}) async-start(s8[12582912]{0:T(1024)(128)(4,1)} %bitcast.325), calls=%async_computation.36 | async-start | bytes 8388608
  832.7 24.0 %slice-start.4 = ((s8[12582912]{0:T(1024)(128)(4,1)}), s8[4194304]{0:T(1024)(128)(4,1)S(1)}, s32[]{:S(2)}) async-start(s8[12582912]{0:T(1024)(128)(4,1)} %bitcast.325), calls=%async_computation.37 | async-start | bytes 8388608
  893.5 11.5 copy-start.70
  910.1 14.9 %copy-start.29 = (bf16[2048,192]{0,1:T(8,128)(2,1)S(1)}, bf16[2048,192]{0,1:T(8,128)(2,1)}, u32[]{:S(2)}) copy-start(bf16[2048,192]{0,1:T(8,128)(2,1)} %copy-done.28) | copy-start | bytes 2359300
  910.2 180.6 %reduce-scatter.20.cloned.1.call-start = ((), (), s32[]{:S(2)}) async-start(), calls=%async_computation.17 | async-start | bytes 1966080 | tf_op jit(solution)/shard_map/reduce_scatter | solution.py:195
  910.2 24.0 %slice-start = ((s8[12582912]{0:T(1024)(128)(4,1)}), s8[4194304]{0:T(1024)(128)(4,1)S(1)}, s32[]{:S(2)}) async-start(s8[12582912]{0:T(1024)(128)(4,1)} %bitcast.323), calls=%async_computation.33 | async-start | bytes 8388608
  910.2 24.0 %slice-start.1 = ((s8[12582912]{0:T(1024)(128)(4,1)}), s8[4194304]{0:T(1024)(128)(4,1)S(1)}, s32[]{:S(2)}) async-start(s8[12582912]{0:T(1024)(128)(4,1)} %bitcast.323), calls=%async_computation.34 | async-start | bytes 8388608
  971.0 11.5 copy-start.68
  987.7 12.3 copy-start.66
  987.7 104.7 %reduce-scatter.24.cloned.1.call-start = ((), (), s32[]{:S(2)}) async-start(), calls=%async_computation.19 | async-start | bytes 1966080 | tf_op jit(solution)/shard_map/reduce_scatter | solution.py:195
  1005.1 104.0 %reduce-scatter.40.cloned.1.call-start = ((), (), s32[]{:S(2)}) async-start(), calls=%async_computation.27 | async-start | bytes 24576
  1005.2 11.2 copy-start.111
  1028.6 12.9 copy-start.36
  1028.6 12.9 copy-start.104
  1041.4 68.6 %reduce-scatter.38.cloned.1.call-start = ((), (), s32[]{:S(2)}) async-start(), calls=%async_computation.26 | async-start | bytes 3538944 | tf_op jit(solution)/shard_map/reduce_scatter | solution.py:245
  1046.6 84.9 %reduce-scatter.36.cloned.1.call-start = ((), (), s32[]{:S(2)}) async-start(), calls=%async_computation.25 | async-start | bytes 3538944 | tf_op jit(solution)/shard_map/reduce_scatter | solution.py:244
  1054.2 94.9 %reduce-scatter.34.cloned.1.call-start = ((), (), s32[]{:S(2)}) async-start(), calls=%async_computation.24 | async-start | bytes 884736 | tf_op jit(solution)/shard_map/reduce_scatter | solution.py:241
  1069.3 97.2 %reduce-scatter.28.cloned.1.call-start = ((), (), s32[]{:S(2)}) async-start(), calls=%async_computation.21 | async-start | bytes 884736 | tf_op jit(solution)/shard_map/reduce_scatter | solution.py:238
  1077.4 106.6 %reduce-scatter.32.cloned.1.call-start = ((), (), s32[]{:S(2)}) async-start(), calls=%async_computation.23 | async-start | bytes 884736 | tf_op jit(solution)/shard_map/reduce_scatter | solution.py:240
  1085.3 116.3 %reduce-scatter.30.cloned.1.call-start = ((), (), s32[]{:S(2)}) async-start(), calls=%async_computation.22 | async-start | bytes 884736 | tf_op jit(solution)/shard_map/reduce_scatter | solution.py:239
  1094.8 180.4 %all-reduce.21.cloned.1.call-start = ((), (), s32[]{:S(2)}) async-start(), calls=%async_computation.28 | async-start | bytes 9437184 | tf_op jit(solution)/shard_map/psum | solution.py:217
  1104.2 248.7 %all-reduce.27.cloned.1.call-start = ((), (), s32[]{:S(2)}) async-start(), calls=%async_computation.31 | async-start | bytes 7077888 | tf_op jit(solution)/shard_map/psum | solution.py:247
  (86 other events, 266.3 us)
Sparse Core Ops, SparseCore 0:
  268.2 173.2 all-reduce.24
  460.5 95.2 all-reduce.28
  559.0 171.6 all-reduce.22
  1104.3 170.8 all-reduce.20
  1277.8 74.9 all-reduce.26
Sparse Core Ops, SparseCore 1:
  270.1 23.2 all-gather.5
  294.7 22.6 all-gather.7
  746.8 27.1 reduce-scatter.17
  776.7 28.1 reduce-scatter.21
  832.7 27.1 reduce-scatter.25
  910.2 26.9 reduce-scatter.15
  987.8 26.9 reduce-scatter.19
  1017.2 28.1 reduce-scatter.23
  1047.4 9.8 reduce-scatter.39
  1059.5 34.6 reduce-scatter.37
  1096.9 34.6 reduce-scatter.35
  1133.8 15.2 reduce-scatter.33
  1151.3 15.2 reduce-scatter.27
  1168.8 15.1 reduce-scatter.31
  1186.4 15.2 reduce-scatter.29
where the time goes:
time: 1380 us; the launch traced here: 1370 us
  waiting for transfers between devices  643 us (47%)
  local copies, waits for them, and re-layouts  268 us (19%)
  matrix products  201 us (15%)
  other arithmetic  135 us (10%)
  blocking collectives  102 us (7%)
  between operations  18.1 us (1%)
    unnamed x280, local copies, waits for them, and re-layouts  179 us
    psum x1, waiting for transfers between devices, body(): lax.psum(jnp.einsum('cf,df->cd', d_hidden, in_full, preferred_element_typ...  175 us
    psum x1, waiting for transfers between devices, body(): resid_mid = resid_in + lax.psum(attn_part, 'tensor')  166 us
    psum x1, waiting for transfers between devices, body(): lax.psum(jnp.dot(active, down_full, preferred_element_type=jnp.float32).a...  79.6 us
    psum x1, waiting for transfers between devices, body(): d_normed_one = lax.psum(d_normed_part, 'tensor')  73.5 us
    reshape x4, local copies, waits for them, and re-layouts, toeplitz(): tiled[:, :row_count * (col_count + row_count - 1)]  57.5 us
    psum x1, waiting for transfers between devices, body(): totals = lax.psum(totals, 'seq')  56.2 us
    reshape x3, other arithmetic, toeplitz(): tiled = tiled.reshape(head_count, row_count * (col_count + row_count))  41.8 us
  transfers between devices with their start and end apart: 20, of which 10 were waited for; matrix products, arithmetic and copies ran while one was open for 28% of the time, Pallas kernels for 0%

commit v1 on v0

v1 whole, which is shorter than its diff:
```python
import functools

import jax
import jax.numpy as jnp
from jax import lax
from jax.experimental import pallas as pl
from jax.experimental.pallas import tpu as pltpu
from jax.sharding import PartitionSpec as P

HEAD = 64
BUCKETS = 32
EPSILON = 1e-06
LIMITS = (12, 16, 23, 32, 46, 64, 91)
LOW = jnp.bfloat16
FULL = jnp.float32
TILE = 128
RANKS = 4
MIX = (0, 2, 1, 3)
IDLE = 1
SPLIT = 1
GELU_A = 0.7978845608028654
GELU_B = 0.044715
KERNEL_MEMORY = 60 * 1024 * 1024


def bucket_of(relative):
    sign_part = jnp.where(relative > 0, 16, 0).astype(jnp.int32)
    distance = jnp.abs(relative)
    far_part = jnp.full(distance.shape, 8, jnp.int32)
    for limit in LIMITS:
        far_part = far_part + (distance >= limit).astype(jnp.int32)
    return sign_part + jnp.where(distance < 8, distance, far_part)


def dot_nn(left, right):
    return lax.dot_general(left, right, (((1,), (0,)), ((), ())), preferred_element_type=FULL)


def dot_nt(left, right):
    return lax.dot_general(left, right, (((1,), (1,)), ((), ())), preferred_element_type=FULL)


def dot_tn(left, right):
    return lax.dot_general(left, right, (((0,), (0,)), ((), ())), preferred_element_type=FULL)


def tile_place(tile, per):
    sub = per // SPLIT
    return ((tile % per) // sub) * (RANKS * sub) + (tile // per) * sub + tile % sub


def tile_at(place, per):
    sub = per // SPLIT
    return ((place // sub) % RANKS) * per + (place // (RANKS * sub)) * sub + place % sub


def params(name_cost=None):
    return pltpu.CompilerParams(vmem_limit_bytes=KERNEL_MEMORY)


def whole_spec(shape):
    return pl.BlockSpec(shape, lambda i, c: tuple(0 for _ in shape))


def project_kernel(heads, per, info, x_ref, gain_ref, w_ref, far_ref, normed, qa, ka, va, kt, vt):
    step = pl.program_id(0)
    rows = x_ref.shape[2]
    x = x_ref[0, 0].astype(FULL)
    scale = lax.rsqrt(jnp.mean(x * x, axis=-1, keepdims=True) + EPSILON)
    xn = (x * scale * gain_ref[...]).astype(LOW)
    normed[...] = xn
    y = dot_nn(xn, w_ref[...])
    row = lax.broadcasted_iota(jnp.int32, (rows, HEAD), 0)
    lane = lax.broadcasted_iota(jnp.int32, (rows, HEAD), 1)
    place = step * (rows // TILE) + row // TILE
    here = tile_at(place, per)
    there = tile_at(lane, per)
    count = RANKS * per
    position = here * TILE + row % TILE
    q_extra = jnp.where(jnp.logical_or(lane == place, lane == count), 1.0, 0.0)
    v_extra = jnp.where(lane == 0, 1.0, 0.0)
    dead = jnp.where(jnp.logical_and(lane == count, position >= info[RANKS]), -1e30, 0.0)
    is_tile = lane < count
    left = jnp.logical_and(is_tile, here < there - 1)
    right = jnp.logical_and(is_tile, here > there + 1)
    width = heads * HEAD
    for h in range(heads):
        k_extra = jnp.where(left, far_ref[0, h], jnp.where(right, far_ref[1, h], dead))
        at = slice(TILE * h, TILE * h + TILE)
        qh = jnp.concatenate([y[:, HEAD * h : HEAD * h + HEAD], q_extra], axis=1)
        kh = jnp.concatenate([y[:, width + HEAD * h : width + HEAD * h + HEAD], k_extra], axis=1)
        vh = jnp.concatenate(
            [y[:, 2 * width + HEAD * h : 2 * width + HEAD * h + HEAD], v_extra], axis=1
        )
        qa[:, at] = qh.astype(LOW)
        ka[:, at] = kh.astype(LOW)
        va[:, at] = vh.astype(LOW)
        kt[at, :] = kh.T.astype(LOW)
        vt[at, :] = vh.T.astype(LOW)


def project(info, x_rel, gain, w_qkv, far, heads, per):
    rows = x_rel.shape[2]
    total = RANKS * SPLIT * rows
    width = x_rel.shape[3]
    row_block = lambda w: pl.BlockSpec((rows, w), lambda i, c: (i, 0))
    col_block = lambda w: pl.BlockSpec((w, rows), lambda i, c: (0, i))
    wide = heads * TILE
    return pl.pallas_call(
        functools.partial(project_kernel, heads, per),
        grid_spec=pltpu.PrefetchScalarGridSpec(
            num_scalar_prefetch=1,
            grid=(RANKS * SPLIT,),
            in_specs=[
                pl.BlockSpec(
                    (1, 1, rows, width), lambda i, c: (c[i % RANKS], i // RANKS, 0, 0)
                ),
                whole_spec(gain.shape),
                whole_spec(w_qkv.shape),
                pl.BlockSpec(memory_space=pltpu.SMEM),
            ],
            out_specs=[
                row_block(width),
                row_block(wide),
                row_block(wide),
                row_block(wide),
                col_block(wide),
                col_block(wide),
            ],
        ),
        out_shape=[
            jax.ShapeDtypeStruct((total, width), LOW),
            jax.ShapeDtypeStruct((total, wide), LOW),
            jax.ShapeDtypeStruct((total, wide), LOW),
            jax.ShapeDtypeStruct((total, wide), LOW),
            jax.ShapeDtypeStruct((wide, total), LOW),
            jax.ShapeDtypeStruct((wide, total), LOW),
        ],
        compiler_params=params(),
        name="project",
    )(info, x_rel, gain, w_qkv, far)


def near_tiles(first_place, tiles, per, visit):
    count = RANKS * per
    for u in range(tiles):
        here = tile_at(first_place + u, per)
        for d in (-1, 0, 1):
            there = here + d
            valid = jnp.logical_and(there >= 0, there < count)
            place = tile_place(jnp.clip(there, 0, count - 1), per)
            rows = pl.ds(pl.multiple_of(place * TILE, TILE), TILE)
            visit(d + 1, rows, slice(u * TILE, u * TILE + TILE), jnp.where(valid, 1.0, 0.0))


def score_block(h, first_place, per, qa, ka, near, s_ref):
    bq = qa.shape[0]
    at = slice(TILE * h, TILE * h + TILE)
    s_ref[h] = dot_nt(ka[:, at], qa[:, at])

    def add(d, rows, cols, valid):
        s_ref[h, rows, cols] = s_ref[h, rows, cols] + near[h, d] * valid

    near_tiles(first_place, bq // TILE, per, add)


def forward_kernel(heads, per, offset, qa, ka, vt, near, mixed, ot, lse, s_ref):
    bq = qa.shape[0]
    first = (pl.program_id(0) + offset) * (bq // TILE)
    for h in range(heads):
        score_block(h, first, per, qa, ka, near, s_ref)
    parts = []
    for h in range(heads):
        s = s_ref[h]
        top = jnp.max(s, axis=0, keepdims=True)
        p = jnp.exp(s - top).astype(LOW)
        o = dot_nn(vt[TILE * h : TILE * h + TILE, :], p)
        total = o[HEAD : HEAD + 1]
        o = o[:HEAD] * (1.0 / total)
        ot[HEAD * h : HEAD * h + HEAD, :] = o
        lse[h : h + 1, :] = top + jnp.log(total)
        parts.append(o.T)
    mixed[...] = jnp.concatenate(parts, axis=1).astype(LOW)


def attend(qa, ka, vt, near, part, bq, per):
    total, wide = ka.shape
    heads = wide // TILE
    span = total // SPLIT
    steps = span // bq
    offset = part * steps
    full = lambda shape: pl.BlockSpec(shape, lambda i: tuple(0 for _ in shape))
    width = heads * HEAD
    return pl.pallas_call(
        functools.partial(forward_kernel, heads, per, offset),
        grid=(steps,),
        in_specs=[
            pl.BlockSpec((bq, wide), lambda i: (i + offset, 0)),
            full(ka.shape),
            full(vt.shape),
            full(near.shape),
        ],
        out_specs=[
            pl.BlockSpec((bq, width), lambda i: (i, 0)),
            pl.BlockSpec((width, bq), lambda i: (0, i)),
            pl.BlockSpec((8, bq), lambda i: (0, i)),
        ],
        out_shape=[
            jax.ShapeDtypeStruct((span, width), LOW),
            jax.ShapeDtypeStruct((width, span), FULL),
            jax.ShapeDtypeStruct((8, span), FULL),
        ],
        scratch_shapes=[pltpu.VMEM((heads, total, bq), FULL)],
        compiler_params=params(),
        name="attend",
    )(qa, ka, vt, near)


def middle_kernel(
    info, x_ref, m0, m1, m2, m3, w_out, gain, w_in, w_down, c_ref,
    ffn, dn, own_resid, g_in, g_down,
):
    step = pl.program_id(0)

    @pl.when(step == 0)
    def _():
        g_in[...] = jnp.zeros_like(g_in)
        g_down[...] = jnp.zeros_like(g_down)

    mixed = jnp.concatenate([m0[...], m1[...], m2[...], m3[...]], axis=1)
    resid = x_ref[0, 0].astype(FULL) + dot_nn(mixed, w_out[...])

    @pl.when(info[step] == 0)
    def _():
        own_resid[...] = resid

    scale = lax.rsqrt(jnp.mean(resid * resid, axis=-1, keepdims=True) + EPSILON)
    normed = (resid * scale * gain[...]).astype(LOW)
    hidden = dot_nn(normed, w_in[...])
    grad = c_ref[0, 0]
    d_active = dot_nt(grad, w_down[...])
    square = hidden * hidden
    th = jnp.tanh(GELU_A * hidden * (1.0 + GELU_B * square))
    half = 0.5 * (1.0 + th)
    active = (hidden * half).astype(LOW)
    slope = half + 0.5 * hidden * (1.0 - th * th) * (GELU_A * (1.0 + (3.0 * GELU_B) * square))
    d_hidden = (d_active * slope).astype(LOW)
    dn[0] = dot_nt(d_hidden, w_in[...]).astype(LOW)
    ffn[0] = dot_nn(active, w_down[...]).astype(LOW)
    g_in[...] += dot_tn(normed, d_hidden)
    g_down[...] += dot_tn(active, grad)


def middle(info, x_rel, pieces, w_out, gain, w_in, w_down, c_rel, part):
    rows, width = x_rel.shape[2:]
    narrow = pieces[0].shape[1]
    hidden = w_in.shape[1]
    rel_block = pl.BlockSpec((1, 1, rows, width), lambda i, c: (c[i], part, 0, 0))
    piece_block = pl.BlockSpec((rows, narrow), lambda i, c: (i, 0))
    out_block = pl.BlockSpec((1, rows, width), lambda i, c: (c[i], 0, 0))
    return pl.pallas_call(
        middle_kernel,
        grid_spec=pltpu.PrefetchScalarGridSpec(
            num_scalar_prefetch=1,
            grid=(RANKS,),
            in_specs=[rel_block]
            + [piece_block] * 4
            + [
                whole_spec(w_out.shape),
                whole_spec(gain.shape),
                whole_spec(w_in.shape),
                whole_spec(w_down.shape),
                rel_block,
            ],
            out_specs=[
                out_block,
                out_block,
                whole_spec((rows, width)),
                whole_spec((width, hidden)),
                whole_spec((hidden, width)),
            ],
        ),
        out_shape=[
            jax.ShapeDtypeStruct((RANKS, rows, width), LOW),
            jax.ShapeDtypeStruct((RANKS, rows, width), LOW),
            jax.ShapeDtypeStruct((rows, width), FULL),
            jax.ShapeDtypeStruct((width, hidden), FULL),
            jax.ShapeDtypeStruct((hidden, width), FULL),
        ],
        compiler_params=params(),
        name="middle",
    )(info, x_rel, *pieces, w_out, gain, w_in, w_down, c_rel)


def backward_kernel(
    heads, per, offset, kc, info, qa, ka, kt, va, d_ref, wo, ot, lse, near,
    dq, dk, dv, d_near, far, g_out, s_ref, ds_ref, dk_acc, dv_acc,
):
    step = pl.program_id(0)
    bq = qa.shape[0]
    total = ka.shape[0]
    count = RANKS * per
    first = (step + offset) * (bq // TILE)

    @pl.when(step == 0)
    def _():
        dk_acc[...] = jnp.zeros_like(dk_acc)
        dv_acc[...] = jnp.zeros_like(dv_acc)
        d_near[...] = jnp.zeros_like(d_near)
        g_out[...] = jnp.zeros_like(g_out)

    d_rows = d_ref[0]
    do = dot_nt(d_rows, wo[...]).astype(LOW)
    do_t = dot_nt(wo[...], d_rows).astype(LOW).astype(FULL)
    g_out[...] += dot_nn(ot[...].astype(LOW), d_rows)
    for h in range(heads):
        score_block(h, first, per, qa, ka, near, s_ref)
    parts = []
    for h in range(heads):
        at = slice(TILE * h, TILE * h + TILE)
        delta = jnp.sum(
            do_t[TILE * h : TILE * h + HEAD] * ot[HEAD * h : HEAD * h + HEAD, :],
            axis=0,
            keepdims=True,
        )
        do_h = do[:, at]
        lse_h = lse[h : h + 1, :]
        dq_t = jnp.zeros((TILE, bq), FULL)
        for c in range(total // kc):
            rows = slice(kc * c, kc * c + kc)
            p = jnp.exp(s_ref[h, rows, :] - lse_h)
            d_p = dot_nt(va[rows, at], do_h)
            d_s = (p * (d_p - delta)).astype(LOW)
            ds_ref[h, rows, :] = d_s
            dv_acc[h, rows, :] += dot_nn(p.astype(LOW), do_h)
            dk_acc[h, rows, :] += dot_nn(d_s, qa[:, at])
            dq_t += dot_nn(kt[at, rows], d_s)
        parts.append(dq_t[:HEAD].T)

        def collect(d, rows, cols, valid):
            d_near[h, d] += ds_ref[h, rows, cols].astype(FULL) * valid

        near_tiles(first, bq // TILE, per, collect)
    dq[...] = jnp.concatenate(parts, axis=1).astype(LOW)

    @pl.when(step == pl.num_programs(0) - 1)
    def _():
        dk[...] = jnp.concatenate([dk_acc[h][:, :HEAD] for h in range(heads)], axis=1).astype(LOW)
        dv[...] = jnp.concatenate([dv_acc[h][:, :HEAD] for h in range(heads)], axis=1).astype(LOW)
        row = lax.broadcasted_iota(jnp.int32, (total, TILE), 0)
        lane = lax.broadcasted_iota(jnp.int32, (total, TILE), 1)
        key_tile = tile_at(row // TILE, per)
        place = lane - HEAD
        is_tile = jnp.logical_and(place >= 0, place < count)
        query_tile = tile_at(jnp.where(is_tile, place, 0), per)
        left = jnp.logical_and(is_tile, key_tile < query_tile - 1)
        right = jnp.logical_and(is_tile, key_tile > query_tile + 1)
        sums = []
        for h in range(heads):
            x = dk_acc[h]
            sums.append(jnp.sum(jnp.where(left, x, 0.0), axis=0, keepdims=True))
            sums.append(jnp.sum(jnp.where(right, x, 0.0), axis=0, keepdims=True))
        sums.append(jnp.zeros((8 - 2 * heads, TILE), FULL))
        far[...] = jnp.concatenate(sums, axis=0)


def attend_back(info, qa, ka, kt, va, d_rel, wo, ot, lse, near, part, kc, per):
    total, wide = ka.shape
    heads = wide // TILE
    rows, model = d_rel.shape[1:]
    bq = rows
    span = total // SPLIT
    steps = span // bq
    offset = part * steps
    width = heads * HEAD
    row_block = lambda w: pl.BlockSpec((bq, w), lambda i, c: (i, 0))
    col_block = lambda w: pl.BlockSpec((w, bq), lambda i, c: (0, i))
    return pl.pallas_call(
        functools.partial(backward_kernel, heads, per, offset, kc),
        grid_spec=pltpu.PrefetchScalarGridSpec(
            num_scalar_prefetch=1,
            grid=(steps,),
            in_specs=[
                pl.BlockSpec((bq, wide), lambda i, c: (i + offset, 0)),
                whole_spec(ka.shape),
                whole_spec(kt.shape),
                whole_spec(va.shape),
                pl.BlockSpec((1, rows, model), lambda i, c: (c[i], 0, 0)),
                whole_spec(wo.shape),
                col_block(width),
                col_block(8),
                whole_spec(near.shape),
            ],
            out_specs=[
                row_block(width),
                whole_spec((total, width)),
                whole_spec((total, width)),
                whole_spec((heads, 3, TILE, TILE)),
                whole_spec((8, TILE)),
                whole_spec((width, model)),
            ],
            scratch_shapes=[
                pltpu.VMEM((heads, total, bq), FULL),
                pltpu.VMEM((heads, total, bq), LOW),
                pltpu.VMEM((heads, total, TILE), FULL),
                pltpu.VMEM((heads, total, TILE), FULL),
            ],
        ),
        out_shape=[
            jax.ShapeDtypeStruct((span, width), LOW),
            jax.ShapeDtypeStruct((total, width), LOW),
            jax.ShapeDtypeStruct((total, width), LOW),
            jax.ShapeDtypeStruct((heads, 3, TILE, TILE), FULL),
            jax.ShapeDtypeStruct((8, TILE), FULL),
            jax.ShapeDtypeStruct((width, model), FULL),
        ],
        compiler_params=params(),
        name="attend_back",
    )(info, qa, ka, kt, va, d_rel, wo, ot, lse, near)


def swap_seq(value, bit):
    return lax.ppermute(value, "seq", [(i, i ^ bit) for i in range(RANKS)])


def gather_seq(value):
    near_one = swap_seq(value, 1)
    far_one = swap_seq(value, 2)
    return (value, near_one, far_one, swap_seq(far_one, 1))


def scatter_seq(parts):
    moved = swap_seq(parts[1::2], 1)
    mine = parts[0].astype(FULL) + moved[0].astype(FULL)
    other = (parts[2].astype(FULL) + moved[1].astype(FULL)).astype(LOW)
    return mine + swap_seq(other, 2).astype(FULL)


def regroup(value, skip):
    pairs = []
    for s in range(RANKS):
        for t in range(RANKS):
            if t != skip:
                pairs.append((s * RANKS + t, s * RANKS + (t ^ MIX[s])))
    return lax.ppermute(value, ("seq", "tensor"), pairs)


def along_tensor(value, pairs):
    return lax.ppermute(value, "tensor", pairs)


def spread(own, rank):
    r1 = along_tensor(own, [(0, 1), (2, 3)])
    l1 = along_tensor(own, [(3, 2), (2, 1)])
    r2 = along_tensor(r1, [(1, 2)])
    l2 = along_tensor(l1, [(2, 1), (1, 0)])
    r3 = along_tensor(r2, [(2, 3)])
    l3 = along_tensor(l2, [(1, 0)])

    def pick(options):
        out = options[0]
        for index in range(1, RANKS):
            out = jnp.where(rank == index, options[index], out)
        return out

    return jnp.stack(
        [pick((own, r1, r2, r3)), pick((l2, l1, own, r1)), pick((l3, l2, l1, own))]
    )


def reduce_weight(partial, axis):
    count = lax.axis_size("dp")
    if count == 2:
        size = partial.shape[axis] // 2
        mine = lax.axis_index("dp")
        keep = lax.dynamic_slice_in_dim(partial, mine * size, size, axis)
        give = lax.dynamic_slice_in_dim(partial, (1 - mine) * size, size, axis)
        keep = keep + lax.ppermute(give.astype(LOW), "dp", [(0, 1), (1, 0)]).astype(FULL)
    else:
        keep = lax.psum_scatter(partial, "dp", scatter_dimension=axis, tiled=True)
    moved = regroup(keep.astype(LOW), IDLE)
    half = moved.shape[0] // 2
    core = lax.axis_index("seq") % 2
    keep = lax.dynamic_slice_in_dim(moved, core * half, half, 0).astype(FULL)
    give = lax.dynamic_slice_in_dim(moved, (1 - core) * half, half, 0)
    keep = (keep + swap_seq(give, 1).astype(FULL)).astype(LOW)
    keep = keep.astype(FULL) + swap_seq(keep, 2).astype(FULL)
    other = swap_seq(keep, 1)
    first = jnp.where(core == 0, keep, other)
    second = jnp.where(core == 0, other, keep)
    return jnp.concatenate([first, second], axis=0)


def gather_dp(value, axis):
    return lax.all_gather(value, "dp", axis=axis, tiled=True)


def body(
    inputs, lengths, gain_attn, w_query, w_key, w_value, w_out, bias_table,
    gain_ffn, w_in, w_down, cotangent,
):
    slots, rows_here, model = inputs.shape
    assert lax.axis_size("seq") == RANKS and lax.axis_size("tensor") == RANKS and slots == 3
    total = RANKS * rows_here
    per = rows_here // TILE
    narrow = w_query.shape[1]
    heads = narrow // HEAD
    rank = lax.axis_index("tensor")
    chunk = lax.axis_index("seq")
    slot = jnp.where(rank == 0, 0, rank - 1)
    length = lax.dynamic_index_in_dim(lengths, slot, 0, keepdims=False)
    order = jnp.bitwise_xor(chunk, jnp.arange(RANKS, dtype=jnp.int32)).astype(jnp.int32)
    info = jnp.concatenate([order, length[None], jnp.zeros((3,), jnp.int32)])
    rows_part = rows_here // SPLIT

    x_own = lax.dynamic_index_in_dim(inputs, slot, 0, keepdims=False)
    c_own = lax.dynamic_index_in_dim(cotangent, slot, 0, keepdims=False)
    position = chunk * rows_here + jnp.arange(rows_here, dtype=jnp.int32)
    live = jnp.logical_and(position < length, rank != IDLE)
    c_own = jnp.where(live[:, None], c_own, jnp.zeros((), LOW))

    w_qkv = gather_dp(regroup(jnp.concatenate([w_query, w_key, w_value], axis=1), None), 0)
    table = gather_dp(regroup(bias_table, None), 0).astype(FULL)
    gain_one = gather_dp(gain_attn, 0).astype(FULL)[None, :]
    gain_two = gather_dp(gain_ffn, 0).astype(FULL)[None, :]
    shape4 = (RANKS, SPLIT, rows_part, model)
    x_rel = jnp.stack(gather_seq(x_own)).reshape(shape4)
    out_mine = gather_dp(regroup(w_out, None), 1)
    in_mine = gather_dp(regroup(w_in, None), 0)
    down_mine = gather_dp(regroup(w_down, None), 1)
    out_rel = jnp.concatenate(gather_seq(out_mine), axis=0)
    c_rel = jnp.stack(gather_seq(c_own)).reshape(shape4)
    out_wide = jnp.pad(
        out_mine.reshape(heads, HEAD, model), ((0, 0), (0, TILE - HEAD), (0, 0))
    ).reshape(heads * TILE, model)

    offset = jnp.arange(TILE, dtype=jnp.int32)
    near_bucket = jnp.stack(
        [bucket_of(TILE * d + offset[:, None] - offset[None, :]) for d in (-1, 0, 1)]
    )
    near = jnp.zeros((heads, 3, TILE, TILE), FULL)
    for b in range(BUCKETS):
        near = near + jnp.where(near_bucket == b, 1.0, 0.0)[None] * table[b][:, None, None, None]
    far_bias = jnp.stack([table[BUCKETS // 2 - 1], table[BUCKETS - 1]])

    normed, qa, ka, va, kt, vt = project(info, x_rel, gain_one, w_qkv, far_bias, heads, per)

    bq = min(512, total // SPLIT)
    attended = [attend(qa, ka, vt, near, part, bq, per) for part in range(SPLIT)]
    mids = [
        middle(
            info, x_rel, gather_seq(attended[part][0]), out_rel, gain_two, in_mine, down_mine,
            c_rel, part,
        )
        for part in range(SPLIT)
    ]
    d_sums = [scatter_seq(mid[1]) for mid in mids]
    ffn_sums = [scatter_seq(mid[0]) for mid in mids]
    g_in = sum(mid[3] for mid in mids)
    g_down = sum(mid[4] for mid in mids)
    c_parts = c_own.reshape(SPLIT, rows_part, model).astype(FULL)
    x_parts = x_own.reshape(SPLIT, rows_part, model).astype(FULL)
    out_parts, d_resids, gain_ffn_part = [], [], 0.0
    for part in range(SPLIT):
        resid = mids[part][2]
        out_parts.append((resid + ffn_sums[part]).astype(LOW))
        scale = lax.rsqrt(jnp.mean(resid * resid, axis=-1, keepdims=True) + EPSILON)
        unit = resid * scale
        along = d_sums[part] * gain_two
        d_resids.append(
            c_parts[part]
            + scale * (along - unit * jnp.mean(along * unit, axis=-1, keepdims=True))
        )
        gain_ffn_part = gain_ffn_part + jnp.sum(d_sums[part] * unit, axis=0)
    d_rels = [jnp.stack(gather_seq(d.astype(LOW))) for d in d_resids]
    outputs = spread(jnp.concatenate(out_parts, axis=0), rank)

    dq, dk, dv, d_near, far, g_out = attend_back(
        info, qa, ka, kt, va, d_rels[0], out_wide, attended[0][1], attended[0][2], near, 0,
        512, per,
    )
    d_qkv = jnp.concatenate([dq, dk, dv], axis=1)
    dn_part = dot_nt(d_qkv, w_qkv).astype(LOW).reshape(SPLIT, RANKS, rows_part, model)
    g_qkv = dot_tn(normed, d_qkv)
    dn_rel = jnp.stack(
        [lax.dynamic_index_in_dim(dn_part, order[r], 1, keepdims=False) for r in range(RANKS)]
    )
    dn_sum = scatter_seq(dn_rel)
    unit = x_parts * lax.rsqrt(jnp.mean(x_parts * x_parts, axis=-1, keepdims=True) + EPSILON)
    scale = lax.rsqrt(jnp.mean(x_parts * x_parts, axis=-1, keepdims=True) + EPSILON)
    along = dn_sum * gain_one
    d_in = jnp.stack(d_resids) + scale * (
        along - unit * jnp.mean(along * unit, axis=-1, keepdims=True)
    )
    gain_attn_part = jnp.sum(dn_sum * unit, axis=(0, 1))
    grad_inputs = spread(d_in.astype(LOW).reshape(rows_here, model), rank)

    d_table = jnp.stack(
        [
            jnp.sum(jnp.where(near_bucket == b, d_near, 0.0), axis=(1, 2, 3))
            for b in range(BUCKETS)
        ]
    )
    far_sum = jnp.sum(far, axis=1)[: 2 * heads].reshape(heads, 2)
    d_table = d_table.at[BUCKETS // 2 - 1].add(far_sum[:, 0]).at[BUCKETS - 1].add(far_sum[:, 1])
    mix = jnp.asarray(MIX, jnp.int32)
    group = jnp.bitwise_xor(rank, lax.dynamic_index_in_dim(mix, chunk, 0, keepdims=False))
    placed = jnp.where(jnp.arange(RANKS)[None, :, None] == group, d_table[:, None, :], 0.0)
    small = jnp.concatenate([gain_attn_part, gain_ffn_part, placed.reshape(-1)])
    small = lax.psum(small, ("dp", "seq", "tensor"))
    mine = lax.axis_index("dp")
    size = gain_attn.shape[0]
    grad_gain_attn = lax.dynamic_slice_in_dim(small, mine * size, size, 0)
    grad_gain_ffn = lax.dynamic_slice_in_dim(small, model + mine * size, size, 0)
    table_all = small[2 * model :].reshape(BUCKETS, RANKS, heads)
    grad_table = lax.dynamic_index_in_dim(table_all, rank, 1, keepdims=False)
    grad_table = lax.dynamic_slice_in_dim(
        grad_table, mine * bias_table.shape[0], bias_table.shape[0], 0
    )

    grad_in = reduce_weight(g_in, 0)
    grad_down = reduce_weight(g_down, 1)
    grad_out = reduce_weight(g_out, 1)
    grad_qkv = reduce_weight(g_qkv, 0)
    return (
        outputs,
        grad_inputs,
        grad_gain_attn,
        grad_qkv[:, :narrow],
        grad_qkv[:, narrow : 2 * narrow],
        grad_qkv[:, 2 * narrow :],
        grad_out,
        grad_table,
        grad_gain_ffn,
        grad_in,
        grad_down,
    )


def solution(mesh):
    in_specs = (
        P("dp", "seq", None),
        P("dp"),
        P("dp"),
        P("dp", "tensor"),
        P("dp", "tensor"),
        P("dp", "tensor"),
        P("tensor", "dp"),
        P("dp", "tensor"),
        P("dp"),
        P("dp", "tensor"),
        P("tensor", "dp"),
        P("dp", "seq", None),
    )
    out_specs = (
        P("dp", "seq", None),
        P("dp", "seq", None),
        P("dp"),
        P("dp", "tensor"),
        P("dp", "tensor"),
        P("dp", "tensor"),
        P("tensor", "dp"),
        P("dp", "tensor"),
        P("dp"),
        P("dp", "tensor"),
        P("tensor", "dp"),
    )
    return jax.shard_map(body, mesh=mesh, in_specs=in_specs, out_specs=out_specs, check_vma=False)
```

time: 1380 us -> 553 us (0.40)
  waiting for transfers between devices: 643 us -> 88.1 us
  local copies, waits for them, and re-layouts: 268 us -> 35.8 us
  matrix products: 201 us -> 9.03 us
  Pallas kernels: 0 us -> 114 us
  starting transfers between devices: 1.65 us -> 115 us
  other arithmetic: 135 us -> 70.3 us
    psum x5 -> x0, waiting for transfers between devices: 550 us -> none  [the longest x1 175 us: body(): lax.psum(jnp.einsum('cf,df->cd', d_hidden, in_full, preferred_element_typ...]
    dot_general x76 -> x2, matrix products: 201 us -> 9.03 us  [the longest x1 6.33 us: dot_nt(): lax.dot_general(left, right, (((1,), (1,)), ((), ())), preferred_element_...]
    unnamed x280 -> x145, local copies, waits for them, and re-layouts: 179 us -> 2.89 us
    ppermute x0 -> x58, starting transfers between devices: none -> 115 us  [the longest x33 62.1 us: swap_seq(): return lax.ppermute(value, 'seq', [(i, i ^ bit) for i in range(RANKS)])]
    pallas_call x0 -> x4, Pallas kernels: none -> 114 us  [the longest x1 48.5 us: attend_back(): pl.pallas_call(functools.partial(backward_kernel, heads, per, offset, kc)...]
    reduce_scatter x12 -> x0, waiting for transfers between devices: 91.7 us -> none  [the longest x1 21.6 us: body(): lax.psum_scatter(totals[7], 'dp', scatter_dimension=0, tiled=True)]
    ppermute x0 -> x58, waiting for transfers between devices: none -> 88.1 us  [the longest x12 36.4 us: along_tensor(): return lax.ppermute(value, 'tensor', pairs)]
    reshape x4 -> x2, local copies, waits for them, and re-layouts: 57.5 us -> 0.33 us  [the longest x1 0.25 us: body(): table_all = small[2 * model:].reshape(BUCKETS, RANKS, heads)]
  transfers between devices with their start and end apart: 20 -> 60, of which waited for: 10 -> 10; matrix products, arithmetic and copies ran while one was open for 28% -> 19% of each run, Pallas kernels for 0% -> 16%
where the time goes in v1:
time: 553 us; the launch traced here: 546 us
  starting transfers between devices  115 us (21%)
  Pallas kernels  114 us (21%)
  blocking collectives  90.6 us (16%)
  waiting for transfers between devices  88.1 us (16%)
  other arithmetic  70.3 us (13%)
  local copies, waits for them, and re-layouts  35.8 us (6%)
  between operations  23.8 us (4%)
  matrix products  9.03 us (2%)
    ppermute x33, starting transfers between devices, swap_seq(): return lax.ppermute(value, 'seq', [(i, i ^ bit) for i in range(RANKS)])  62.1 us
    pallas_call x1, Pallas kernels, attend_back(): pl.pallas_call(functools.partial(backward_kernel, heads, per, offset, kc)...  48.5 us
    all_gather x5, blocking collectives, gather_dp(): return lax.all_gather(value, 'dp', axis=axis, tiled=True)  46.5 us
    psum x1, blocking collectives, body(): small = lax.psum(small, ('dp', 'seq', 'tensor'))  44.1 us
    ppermute x12, waiting for transfers between devices, along_tensor(): return lax.ppermute(value, 'tensor', pairs)  36.4 us
    ppermute x33, waiting for transfers between devices, swap_seq(): return lax.ppermute(value, 'seq', [(i, i ^ bit) for i in range(RANKS)])  33.6 us
    pallas_call x1, Pallas kernels, middle(): pl.pallas_call(middle_kernel, grid_spec=pltpu.PrefetchScalarGridSpec(num_...  28.6 us
    ppermute x9, starting transfers between devices, regroup(): return lax.ppermute(value, ('seq', 'tensor'), pairs)  26.7 us
  transfers between devices with their start and end apart: 60, of which 10 were waited for; matrix products, arithmetic and copies ran while one was open for 19% of the time, Pallas kernels for 16%

profile of v1, /device:TPU:0, one launch (start us, length us, event | category | flops | bytes accessed | tf_op | source)
XLA Modules:
  0.0 546.4 jit_solution(6793351212050844796)
XLA Ops:
  8.8 3.0 collective-permute-start.1
  14.4 5.2 collective-permute-start.3
  19.6 5.9 %collective-permute-start.12 = (bf16[384,768]{1,0:T(8,128)(2,1)}, bf16[384,768]{1,0:T(8,128)(2,1)}, u32[]{:S(2)}, u32[]{:S(2)}) collective-permute-start(bf16[384,768]{1,0:T(8,128)(2,1)} %param.26), channel_id=1, source_target_pairs={{0,0},{1,1},{2,2},{3,3},{4,6},{5,7},{6,4},{7,5},{8,9},{9,8},{10,11... | collective-permute-start | bytes 1769480 | tf_op jit(solution)/shard_map/ppermute | solution.py:445
  35.0 4.3 all-gather
  39.4 2.2 bitcast_select_fusion
  42.1 4.4 all-gather.1
  48.3 5.9 %collective-permute-start.13 = (bf16[768,384]{1,0:T(8,128)(2,1)}, bf16[768,384]{1,0:T(8,128)(2,1)}, u32[]{:S(2)}, u32[]{:S(2)}) collective-permute-start(bf16[768,384]{1,0:T(8,128)(2,1)} %param.27), channel_id=1, source_target_pairs={{0,0},{1,1},{2,2},{3,3},{4,6},{5,7},{6,4},{7,5},{8,9},{9,8},{10,11... | collective-permute-start | bytes 1769480 | tf_op jit(solution)/shard_map/ppermute | solution.py:445
  54.4 5.3 multiply_add_fusion.near
  60.3 27.2 %all_gather.22.w_ref = bf16[768,576]{1,0:T(8,128)(2,1)} all-gather(bf16[384,576]{1,0:T(8,128)(2,1)} %collective-permute-done.3), channel_id=1, replica_groups=mesh['dp'=2,'seq'=4,'tensor'=4] {'dp'}, dimensions={0}, use_global_device_ids=true | all-gather | bytes 1327104 | tf_op jit(solution)/shard_map/all_gather | solution.py:495
  87.5 1.9 maximum_bitcast_fusion.x_ref
  89.4 11.2 %project.1 = (bf16[2048,768]{1,0:T(8,128)(2,1)}, bf16[2048,384]{1,0:T(8,128)(2,1)}, bf16[2048,384]{1,0:T(8,128)(2,1)}, bf16[2048,384]{1,0:T(8,128)(2,1)}, bf16[3...) custom-call(s32[8]{0:T(128)} %pad_add_fusion.1.info, bf16[4,1,512,768]{3,2,1,0:T(8,128)(2,1)} %maximum_bitcast_fusion.x_ref, ...), custom_call_target="tpu_custom_call" | custom-call | tf_op jit(solution)/shard_map/project/pallas_call | solution.py:109
  100.6 25.4 %attend.1 = (bf16[2048,192]{1,0:T(8,128)(2,1)}, f32[192,2048]{1,0:T(8,128)}, f32[8,2048]{1,0:T(8,128)}) custom-call(bf16[2048,384]{1,0:T(8,128)(2,1)} %get-tuple-element.55.qa, bf16[2048,384]{1,0:T(8,128)(2,1)} %get-tuple-element.56.ka, bf16[384,2048]{1,0:T(8,128)(2,1)} %get-tuple-element.57.vt, f32[3,3,128,128]{3,2,1,0:T(8,128)} %multiply_add_fusion.near), custom_call_target="tpu_custom_call" | custom-call | tf_op jit(solution)/shard_map/attend/pallas_call | solution.py:194
  129.0 6.0 %all_gather.24 = bf16[192,768]{1,0:T(8,128)(2,1)S(1)} all-gather(bf16[192,384]{1,0:T(8,128)(2,1)} %collective-permute-done.8), channel_id=1, replica_groups=mesh['dp'=2,'seq'=4,'tensor'=4] {'dp'}, dimensions={1}, use_global_device_ids=true | all-gather | bytes 442368 | tf_op jit(solution)/shard_map/all_gather | solution.py:495
  135.0 12.3 %collective-permute-start.10 = (bf16[192,768]{1,0:T(8,128)(2,1)S(1)}, bf16[192,768]{1,0:T(8,128)(2,1)}, u32[]{:S(2)}, u32[]{:S(2)}) collective-permute-start(bf16[192,768]{1,0:T(8,128)(2,1)S(1)} %all_gather.24), channel_id=1, source_target_pairs={{0,8},{4,12},{8,0},{12,4},{1,9},{5,13},{9,1},{13,5},{2,10},{6,14},... | collective-permute-start | bytes 884744 | tf_op jit(solution)/shard_map/ppermute | solution.py:423
  147.9 5.3 collective-permute-done.10
  154.4 4.5 all-gather.2
  160.9 2.1 pad_maximum_fusion.5.w_out
  163.0 3.0 maximum_bitcast_fusion.1.c_ref
  167.3 2.2 copy.104.m1
  169.5 2.3 copy.106.m3
  171.8 28.6 %middle.1 = (bf16[4,512,768]{2,1,0:T(8,128)(2,1)}, bf16[4,512,768]{2,1,0:T(8,128)(2,1)}, f32[512,768]{1,0:T(8,128)}, f32[768,768]{1,0:T(8,128)}, f32[768,768]{1,0:T(8,128)}) custom-call(s32[8]{0:T(128)} %pad_add_fusion.1.info, bf16[4,1,512,768]{3,2,1,0:T(8,128)(2,1)} %maximum_bitcast_fusion.x_ref, bf16[2048,192]{1,0:T(8,128)(2,1)} %get-tuple-element.58.m0, ...), custom_call_target="tpu_custom_call" | custom-call | tf_op jit(solution)/shard_map/middle/pallas_call | solution.py:261
  200.4 2.2 dynamic-slice_convert_fusion
  203.2 2.7 slice.256
  208.9 1.7 slice.251
  210.8 8.2 %collective-permute-done.53 = bf16[768,384]{1,0:T(8,128)(2,1)S(1)} collective-permute-done((bf16[768,384]{1,0:T(8,128)(2,1)}, bf16[768,384]{1,0:T(8,128)(2,1)S(1)}, u32[]{:S(2)}, u32[]{:S(2)}) %collective-permute-start.53) | collective-permute-done | bytes 589856 | tf_op jit(solution)/shard_map/ppermute | solution.py:478
  220.1 9.9 %collective-permute-done.48 = bf16[384,768]{1,0:T(8,128)(2,1)S(1)} collective-permute-done((bf16[384,768]{1,0:T(8,128)(2,1)S(1)}, bf16[384,768]{1,0:T(8,128)(2,1)S(1)}, u32[]{:S(2)}, u32[]{:S(2)}) %collective-permute-start.48) | collective-permute-done | bytes 589856 | tf_op jit(solution)/shard_map/ppermute | solution.py:478
  230.9 3.0 collective-permute-start.55
  234.1 2.4 collective-permute-start.26
  236.6 9.9 %collective-permute-start.50 = (bf16[192,768]{1,0:T(8,128)(2,1)S(1)}, bf16[192,768]{1,0:T(8,128)(2,1)S(1)}, u32[]{:S(2)}, u32[]{:S(2)}) collective-permute-start(bf16[192,768]{1,0:T(8,128)(2,1)S(1)} %constant_dynamic-slice_fusion.1), channel_id=1, source_target_pairs={{0,4},{4,0},{8,12},{12,8},{1,5},{5,1},{9,13},{13,9},{2,6},{6,2},{1... | collective-permute-start | bytes 884744 | tf_op jit(solution)/shard_map/ppermute | solution.py:423
  246.6 2.6 collective-permute-start.56
  249.6 2.1 collective-permute-start.51
  251.6 3.3 collective-permute-done.26
  255.7 22.4 %collective-permute-done.18 = bf16[512,768]{1,0:T(8,128)(2,1)S(1)} collective-permute-done((bf16[512,768]{1,0:T(8,128)(2,1)S(1)}, bf16[512,768]{1,0:T(8,128)(2,1)S(1)}, u32[]{:S(2)}, u32[]{:S(2)}) %collective-permute-start.18) | collective-permute-done | bytes 786464 | tf_op jit(solution)/shard_map/ppermute | solution.py:423
  278.1 3.2 fusion.52
  281.3 1.9 collective-permute-start.28
  298.4 5.3 collective-permute-start.19
  310.3 9.9 %collective-permute-done.19 = bf16[512,768]{1,0:T(8,128)(2,1)} collective-permute-done((bf16[512,768]{1,0:T(8,128)(2,1)S(1)}, bf16[512,768]{1,0:T(8,128)(2,1)}, u32[]{:S(2)}, u32[]{:S(2)}) %collective-permute-start.19) | collective-permute-done | bytes 786464 | tf_op jit(solution)/shard_map/ppermute | solution.py:449
  323.1 3.0 pad_maximum_fusion.d_ref
  326.1 48.5 %attend_back.1 = (bf16[2048,192]{1,0:T(8,128)(2,1)}, bf16[2048,192]{1,0:T(8,128)(2,1)}, bf16[2048,192]{1,0:T(8,128)(2,1)}, f32[3,3,128,128]{3,2,1,0:T(8,128)}, f32[8,128]{1,0:T(8,128)}, /*index=5*/f32[192,768]{1,0:T(8,128)}) custom-call(s32[8]{0:T(128)} %pad_add_fusion.1.info, bf16[2048,384]{1,0:T(8,128)(2,1)} %get-tuple-element.55.qa, ...), custom_call_target="tpu_custom_call" | custom-call | tf_op jit(solution)/shard_map/attend_back/pallas_call | solution.py:378
  374.5 1.6 dynamic-slice_convert_fusion.3
  376.6 6.3 %convolution_convert_fusion = bf16[2048,768]{1,0:T(8,128)(2,1)} fusion(bf16[768,576]{1,0:T(8,128)(2,1)S(1)} %copy-done.2, bf16[2048,192]{1,0:T(8,128)(2,1)} %get-tuple-element.68, bf16[2048,192]{1,0:T(8,128)(2,1)} %get-tuple-element.67, bf16[2048,192]{1,0:T(8,128)(2,1)} %get-tuple-element.66), kind=kOutput, calls=%fused_computation | convolution fusion | flops 1820590080 | bytes 6389760 | tf_op jit(solution)/shard_map/dot_general | solution.py:40
  382.9 2.7 fusion.12
  387.7 1.7 collective-permute-start.38
  389.5 1.8 constant_dynamic-slice_fusion.7
  393.3 2.0 select_reduce_fusion.18
  395.3 2.2 select_reduce_fusion
  397.5 2.9 stack.239
  403.1 14.4 %collective-permute-start.45 = (bf16[96,384]{1,0:T(8,128)(2,1)S(1)}, bf16[96,384]{1,0:T(8,128)(2,1)S(1)}, u32[]{:S(2)}, u32[]{:S(2)}) collective-permute-start(bf16[96,384]{1,0:T(8,128)(2,1)S(1)} %constant_dynamic-slice_fusion.3), channel_id=1, source_target_pairs={{0,4},{4,0},{8,12},{12,8},{1,5},{5,1},{9,13},{13,9},{2,6},{6,2},{1... | collective-permute-start | bytes 221192 | tf_op jit(solution)/shard_map/ppermute | solution.py:423
  417.5 2.2 fusion.15
  419.7 1.9 add_convert_fusion.5
  421.6 5.0 collective-permute-start.39
  426.9 1.6 collective-permute-start.21
  431.2 6.7 %collective-permute-start.40 = (bf16[192,576]{0,1:T(8,128)(2,1)S(1)}, bf16[192,576]{0,1:T(8,128)(2,1)S(1)}, u32[]{:S(2)}, u32[]{:S(2)}) collective-permute-start(bf16[192,576]{0,1:T(8,128)(2,1)S(1)} %constant_dynamic-slice_fusion.4), channel_id=1, source_target_pairs={{0,4},{4,0},{8,12},{12,8},{1,5},{5,1},{9,13},{13,9},{2,6},{6,2},{1... | collective-permute-start | bytes 663560 | tf_op jit(solution)/shard_map/ppermute | solution.py:423
  437.9 2.2 collective-permute-done.31
  440.2 2.4 fusion.8
  442.6 2.3 fusion.16
  444.8 2.2 collective-permute-start.32
  452.2 9.7 %collective-permute-done.32 = bf16[512,768]{1,0:T(8,128)(2,1)} collective-permute-done((bf16[512,768]{1,0:T(8,128)(2,1)S(1)}, bf16[512,768]{1,0:T(8,128)(2,1)}, u32[]{:S(2)}, u32[]{:S(2)}) %collective-permute-start.32) | collective-permute-done | bytes 786464 | tf_op jit(solution)/shard_map/ppermute | solution.py:449
  465.1 2.1 select_bitcast_fusion.4
  467.3 1.7 pad_maximum_fusion.2
  470.7 16.7 %collective-permute-done.36 = bf16[512,768]{1,0:T(8,128)(2,1)} collective-permute-done((bf16[512,768]{1,0:T(8,128)(2,1)}, bf16[512,768]{1,0:T(8,128)(2,1)}, u32[]{:S(2)}, u32[]{:S(2)}) %collective-permute-start.36) | collective-permute-done | bytes 786464 | tf_op jit(solution)/shard_map/ppermute | solution.py:449
  490.0 44.1 %psum.7 = f32[1920]{0:T(1024)S(1)} all-reduce(f32[1920]{0:T(1024)S(1)} %pad_maximum_fusion.13), channel_id=1, replica_groups=mesh['dp'=2,'seq'=4,'tensor'=4] {'dp','seq','tensor'}, use_global_device_ids=true, to_apply=%region_39.40 | all-reduce | flops 1920 | bytes 15360 | tf_op jit(solution)/shard_map/psum | solution.py:610
  535.6 2.1 select_bitcast_fusion.1
  537.8 1.7 pad_maximum_fusion.4
  (326 shorter events, 72.0 us)
Async XLA Ops:
  7.2 164.6 %all-gather.6.cloned.1.call-start = ((), (), s32[]{:S(2)}) async-start(), calls=%async_computation | async-start | bytes 1769472 | tf_op jit(solution)/shard_map/all_gather | solution.py:495
  8.8 45.5 %collective-permute-start.1 = (bf16[512,768]{1,0:T(8,128)(2,1)S(1)}, bf16[512,768]{1,0:T(8,128)(2,1)S(1)}, u32[]{:S(2)}, u32[]{:S(2)}) collective-permute-start(bf16[512,768]{1,0:T(8,128)(2,1)S(1)} %bitcast.132), channel_id=1, source_target_pairs={{0,8},{4,12},{8,0},{12,4},{1,9},{5,13},{9,1},{13,5},{2,10},{6,14},... | collective-permute-start | bytes 2359304 | tf_op jit(solution)/shard_map/ppermute | solution.py:423
  11.8 75.8 %collective-permute-start = (bf16[512,768]{1,0:T(8,128)(2,1)S(1)}, bf16[512,768]{1,0:T(8,128)(2,1)S(1)}, u32[]{:S(2)}, u32[]{:S(2)}) collective-permute-start(bf16[512,768]{1,0:T(8,128)(2,1)S(1)} %bitcast.133), channel_id=1, source_target_pairs={{0,4},{4,0},{8,12},{12,8},{1,5},{5,1},{9,13},{13,9},{2,6},{6,2},{1... | collective-permute-start | bytes 2359304 | tf_op jit(solution)/shard_map/ppermute | solution.py:423
  11.8 30.4 %collective-permute-start.4 = (bf16[16,3]{0,1:T(4,128)(2,1)S(1)}, bf16[16,3]{0,1:T(4,128)(2,1)}, u32[]{:S(2)}, u32[]{:S(2)}) collective-permute-start(bf16[16,3]{0,1:T(4,128)(2,1)S(1)} %copy-done.67), channel_id=1, source_target_pairs={{0,0},{1,1},{2,2},{3,3},{4,6},{5,7},{6,4},{7,5},{8,9},{9,8},{10,11... | collective-permute-start | bytes 296 | tf_op jit(solution)/shard_map/ppermute | solution.py:445
  14.4 45.9 %collective-permute-start.3 = (bf16[384,576]{1,0:T(8,128)(2,1)}, bf16[384,576]{1,0:T(8,128)(2,1)}, u32[]{:S(2)}, u32[]{:S(2)}) collective-permute-start(bf16[384,576]{1,0:T(8,128)(2,1)} %pad_maximum_fusion.10), channel_id=1, source_target_pairs={{0,0},{1,1},{2,2},{3,3},{4,6},{5,7},{6,4},{7,5},{8,9},{9,8},{10,11... | collective-permute-start | bytes 1327112 | tf_op jit(solution)/shard_map/ppermute | solution.py:445
  19.6 28.7 %collective-permute-start.12 = (bf16[384,768]{1,0:T(8,128)(2,1)}, bf16[384,768]{1,0:T(8,128)(2,1)}, u32[]{:S(2)}, u32[]{:S(2)}) collective-permute-start(bf16[384,768]{1,0:T(8,128)(2,1)} %param.26), channel_id=1, source_target_pairs={{0,0},{1,1},{2,2},{3,3},{4,6},{5,7},{6,4},{7,5},{8,9},{9,8},{10,11... | collective-permute-start | bytes 1769480 | tf_op jit(solution)/shard_map/ppermute | solution.py:445
  35.0 124.5 %copy-start.56 = (pred[512]{0:T(512)(128)(4,1)}, pred[512]{0:T(512)(128)(4,1)S(1)}, u32[]{:S(2)}) copy-start(pred[512]{0:T(512)(128)(4,1)S(1)} %fusion.49) | copy-start | bytes 1540
  42.1 105.2 %collective-permute-start.15 = (bf16[512,768]{1,0:T(8,128)(2,1)}, bf16[512,768]{1,0:T(8,128)(2,1)S(1)}, u32[]{:S(2)}, u32[]{:S(2)}) collective-permute-start(bf16[512,768]{1,0:T(8,128)(2,1)} %bitcast_select_fusion), channel_id=1, source_target_pairs={{0,8},{4,12},{8,0},{12,4},{1,9},{5,13},{9,1},{13,5},{2,10},{6,14},... | collective-permute-start | bytes 2359304 | tf_op jit(solution)/shard_map/ppermute | solution.py:423
  48.3 80.7 %collective-permute-start.13 = (bf16[768,384]{1,0:T(8,128)(2,1)}, bf16[768,384]{1,0:T(8,128)(2,1)}, u32[]{:S(2)}, u32[]{:S(2)}) collective-permute-start(bf16[768,384]{1,0:T(8,128)(2,1)} %param.27), channel_id=1, source_target_pairs={{0,0},{1,1},{2,2},{3,3},{4,6},{5,7},{6,4},{7,5},{8,9},{9,8},{10,11... | collective-permute-start | bytes 1769480 | tf_op jit(solution)/shard_map/ppermute | solution.py:445
  54.2 117.6 %all-gather.8.cloned.1.call-start = ((), (), s32[]{:S(2)}) async-start(), calls=%async_computation.1 | async-start | bytes 1769472 | tf_op jit(solution)/shard_map/all_gather | solution.py:495
  54.3 33.2 %collective-permute-start.2 = (bf16[512,768]{1,0:T(8,128)(2,1)S(1)}, bf16[512,768]{1,0:T(8,128)(2,1)S(1)}, u32[]{:S(2)}, u32[]{:S(2)}) collective-permute-start(bf16[512,768]{1,0:T(8,128)(2,1)S(1)} %collective-permute-done.1), channel_id=1, source_target_pairs={{0,4},{4,0},{8,12},{12,8},{1,5},{5,1},{9,13},{13,9},{2,6},{6,2},{1... | collective-permute-start | bytes 2359304 | tf_op jit(solution)/shard_map/ppermute | solution.py:423
  127.6 25.6 %collective-permute-start.6 = (bf16[2048,192]{0,1:T(8,128)(2,1)S(1)}, bf16[2048,192]{0,1:T(8,128)(2,1)S(1)}, u32[]{:S(2)}, u32[]{:S(2)}) collective-permute-start(bf16[2048,192]{0,1:T(8,128)(2,1)S(1)} %copy.101), channel_id=1, source_target_pairs={{0,8},{4,12},{8,0},{12,4},{1,9},{5,13},{9,1},{13,5},{2,10},{6,14},... | collective-permute-start | bytes 2359304 | tf_op jit(solution)/shard_map/ppermute | solution.py:423
  127.6 1.3 collective-permute-start.8
  135.0 18.2 %collective-permute-start.10 = (bf16[192,768]{1,0:T(8,128)(2,1)S(1)}, bf16[192,768]{1,0:T(8,128)(2,1)}, u32[]{:S(2)}, u32[]{:S(2)}) collective-permute-start(bf16[192,768]{1,0:T(8,128)(2,1)S(1)} %all_gather.24), channel_id=1, source_target_pairs={{0,8},{4,12},{8,0},{12,4},{1,9},{5,13},{9,1},{13,5},{2,10},{6,14},... | collective-permute-start | bytes 884744 | tf_op jit(solution)/shard_map/ppermute | solution.py:423
  147.3 15.7 %collective-permute-start.14 = (bf16[512,768]{1,0:T(8,128)(2,1)}, bf16[512,768]{1,0:T(8,128)(2,1)}, u32[]{:S(2)}, u32[]{:S(2)}) collective-permute-start(bf16[512,768]{1,0:T(8,128)(2,1)} %bitcast_select_fusion), channel_id=1, source_target_pairs={{0,4},{4,0},{8,12},{12,8},{1,5},{5,1},{9,13},{13,9},{2,6},{6,2},{1... | collective-permute-start | bytes 2359304 | tf_op jit(solution)/shard_map/ppermute | solution.py:423
  147.4 15.7 %collective-permute-start.16 = (bf16[512,768]{1,0:T(8,128)(2,1)S(1)}, bf16[512,768]{1,0:T(8,128)(2,1)}, u32[]{:S(2)}, u32[]{:S(2)}) collective-permute-start(bf16[512,768]{1,0:T(8,128)(2,1)S(1)} %collective-permute-done.15), channel_id=1, source_target_pairs={{0,4},{4,0},{8,12},{12,8},{1,5},{5,1},{9,13},{13,9},{2,6},{6,2},{1... | collective-permute-start | bytes 2359304 | tf_op jit(solution)/shard_map/ppermute | solution.py:423
  147.9 5.9 %collective-permute-start.9 = (bf16[192,768]{1,0:T(8,128)(2,1)S(1)}, bf16[192,768]{1,0:T(8,128)(2,1)S(1)}, u32[]{:S(2)}, u32[]{:S(2)}) collective-permute-start(bf16[192,768]{1,0:T(8,128)(2,1)S(1)} %all_gather.24), channel_id=1, source_target_pairs={{0,4},{4,0},{8,12},{12,8},{1,5},{5,1},{9,13},{13,9},{2,6},{6,2},{1... | collective-permute-start | bytes 884744 | tf_op jit(solution)/shard_map/ppermute | solution.py:423
  153.2 14.1 %collective-permute-start.5 = (bf16[2048,192]{0,1:T(8,128)(2,1)S(1)}, bf16[2048,192]{0,1:T(8,128)(2,1)}, u32[]{:S(2)}, u32[]{:S(2)}) collective-permute-start(bf16[2048,192]{0,1:T(8,128)(2,1)S(1)} %copy.101), channel_id=1, source_target_pairs={{0,4},{4,0},{8,12},{12,8},{1,5},{5,1},{9,13},{13,9},{2,6},{6,2},{1... | collective-permute-start | bytes 2359304 | tf_op jit(solution)/shard_map/ppermute | solution.py:423
  153.2 16.3 %collective-permute-start.7 = (bf16[2048,192]{0,1:T(8,128)(2,1)S(1)}, bf16[2048,192]{0,1:T(8,128)(2,1)}, u32[]{:S(2)}, u32[]{:S(2)}) collective-permute-start(bf16[2048,192]{0,1:T(8,128)(2,1)S(1)} %collective-permute-done.6), channel_id=1, source_target_pairs={{0,4},{4,0},{8,12},{12,8},{1,5},{5,1},{9,13},{13,9},{2,6},{6,2},{1... | collective-permute-start | bytes 2359304 | tf_op jit(solution)/shard_map/ppermute | solution.py:423
  154.4 6.4 %collective-permute-start.11 = (bf16[192,768]{1,0:T(8,128)(2,1)}, bf16[192,768]{1,0:T(8,128)(2,1)}, u32[]{:S(2)}, u32[]{:S(2)}) collective-permute-start(bf16[192,768]{1,0:T(8,128)(2,1)} %collective-permute-done.10), channel_id=1, source_target_pairs={{0,4},{4,0},{8,12},{12,8},{1,5},{5,1},{9,13},{13,9},{2,6},{6,2},{1... | collective-permute-start | bytes 884744 | tf_op jit(solution)/shard_map/ppermute | solution.py:423
  202.5 16.5 %collective-permute-start.53 = (bf16[768,384]{1,0:T(8,128)(2,1)}, bf16[768,384]{1,0:T(8,128)(2,1)S(1)}, u32[]{:S(2)}, u32[]{:S(2)}) collective-permute-start(bf16[768,384]{1,0:T(8,128)(2,1)} %dynamic-slice_convert_fusion), channel_id=1, source_target_pairs={{0,16},{16,0},{1,17},{17,1},{2,18},{18,2},{3,19},{19,3},{4,20},{20... | collective-permute-start | bytes 1769480 | tf_op jit(solution)/shard_map/ppermute | solution.py:478
  205.8 28.0 %collective-permute-start.25 = (bf16[2,512,768]{2,1,0:T(8,128)(2,1)}, bf16[2,512,768]{2,1,0:T(8,128)(2,1)S(1)}, u32[]{:S(2)}, u32[]{:S(2)}) collective-permute-start(bf16[2,512,768]{2,1,0:T(8,128)(2,1)} %slice.256), channel_id=1, source_target_pairs={{0,4},{4,0},{8,12},{12,8},{1,5},{5,1},{9,13},{13,9},{2,6},{6,2},{1... | collective-permute-start | bytes 4718600 | tf_op jit(solution)/shard_map/ppermute | solution.py:423
  207.4 22.6 %collective-permute-start.48 = (bf16[384,768]{1,0:T(8,128)(2,1)S(1)}, bf16[384,768]{1,0:T(8,128)(2,1)S(1)}, u32[]{:S(2)}, u32[]{:S(2)}) collective-permute-start(bf16[384,768]{1,0:T(8,128)(2,1)S(1)} %dynamic-slice_convert_fusion.1), channel_id=1, source_target_pairs={{0,16},{16,0},{1,17},{17,1},{2,18},{18,2},{3,19},{19,3},{4,20},{20... | collective-permute-start | bytes 1769480 | tf_op jit(solution)/shard_map/ppermute | solution.py:478
  210.5 38.6 %collective-permute-start.17 = (bf16[2,512,768]{2,1,0:T(8,128)(2,1)S(1)}, bf16[2,512,768]{2,1,0:T(8,128)(2,1)S(1)}, u32[]{:S(2)}, u32[]{:S(2)}) collective-permute-start(bf16[2,512,768]{2,1,0:T(8,128)(2,1)S(1)} %slice.251), channel_id=1, source_target_pairs={{0,4},{4,0},{8,12},{12,8},{1,5},{5,1},{9,13},{13,9},{2,6},{6,2},{1... | collective-permute-start | bytes 4718600 | tf_op jit(solution)/shard_map/ppermute | solution.py:423
  219.2 11.6 %collective-permute-start.54 = (bf16[768,384]{1,0:T(8,128)(2,1)S(1)}, bf16[768,384]{1,0:T(8,128)(2,1)S(1)}, u32[]{:S(2)}, u32[]{:S(2)}) collective-permute-start(bf16[768,384]{1,0:T(8,128)(2,1)S(1)} %add_convert_fusion.3), channel_id=1, source_target_pairs={{0,0},{2,2},{3,3},{4,6},{6,4},{7,5},{8,9},{10,11},{11,10},{12,15},... | collective-permute-start | bytes 1769480 | tf_op jit(solution)/shard_map/ppermute | solution.py:445
  230.1 6.4 %collective-permute-start.49 = (bf16[384,768]{1,0:T(8,128)(2,1)S(1)}, bf16[384,768]{1,0:T(8,128)(2,1)S(1)}, u32[]{:S(2)}, u32[]{:S(2)}) collective-permute-start(bf16[384,768]{1,0:T(8,128)(2,1)S(1)} %add_convert_fusion.4), channel_id=1, source_target_pairs={{0,0},{2,2},{3,3},{4,6},{6,4},{7,5},{8,9},{10,11},{11,10},{12,15},... | collective-permute-start | bytes 1769480 | tf_op jit(solution)/shard_map/ppermute | solution.py:445
  230.9 15.6 %collective-permute-start.55 = (bf16[384,384]{1,0:T(8,128)(2,1)S(1)}, bf16[384,384]{1,0:T(8,128)(2,1)S(1)}, u32[]{:S(2)}, u32[]{:S(2)}) collective-permute-start(bf16[384,384]{1,0:T(8,128)(2,1)S(1)} %constant_dynamic-slice_fusion), channel_id=1, source_target_pairs={{0,4},{4,0},{8,12},{12,8},{1,5},{5,1},{9,13},{13,9},{2,6},{6,2},{1... | collective-permute-start | bytes 884744 | tf_op jit(solution)/shard_map/ppermute | solution.py:423
  234.1 20.8 %collective-permute-start.26 = (bf16[512,768]{1,0:T(8,128)(2,1)S(1)}, bf16[512,768]{1,0:T(8,128)(2,1)S(1)}, u32[]{:S(2)}, u32[]{:S(2)}) collective-permute-start(bf16[512,768]{1,0:T(8,128)(2,1)S(1)} %fusion.14), channel_id=1, source_target_pairs={{0,8},{4,12},{8,0},{12,4},{1,9},{5,13},{9,1},{13,5},{2,10},{6,14},... | collective-permute-start | bytes 2359304 | tf_op jit(solution)/shard_map/ppermute | solution.py:423
  236.6 12.9 %collective-permute-start.50 = (bf16[192,768]{1,0:T(8,128)(2,1)S(1)}, bf16[192,768]{1,0:T(8,128)(2,1)S(1)}, u32[]{:S(2)}, u32[]{:S(2)}) collective-permute-start(bf16[192,768]{1,0:T(8,128)(2,1)S(1)} %constant_dynamic-slice_fusion.1), channel_id=1, source_target_pairs={{0,4},{4,0},{8,12},{12,8},{1,5},{5,1},{9,13},{13,9},{2,6},{6,2},{1... | collective-permute-start | bytes 884744 | tf_op jit(solution)/shard_map/ppermute | solution.py:423
  246.6 36.7 %copy-start.8 = (bf16[384,384]{1,0:T(8,128)(2,1)}, bf16[384,384]{1,0:T(8,128)(2,1)S(1)}, u32[]{:S(2)}) copy-start(bf16[384,384]{1,0:T(8,128)(2,1)S(1)} %add_convert_fusion.6) | copy-start | bytes 884740
  246.6 36.7 %collective-permute-start.56 = (bf16[384,384]{1,0:T(8,128)(2,1)S(1)}, bf16[384,384]{1,0:T(8,128)(2,1)S(1)}, u32[]{:S(2)}, u32[]{:S(2)}) collective-permute-start(bf16[384,384]{1,0:T(8,128)(2,1)S(1)} %add_convert_fusion.6), channel_id=1, source_target_pairs={{0,8},{4,12},{8,0},{12,4},{1,9},{5,13},{9,1},{13,5},{2,10},{6,14},... | collective-permute-start | bytes 884744 | tf_op jit(solution)/shard_map/ppermute | solution.py:423
  249.3 28.8 %collective-permute-start.18 = (bf16[512,768]{1,0:T(8,128)(2,1)S(1)}, bf16[512,768]{1,0:T(8,128)(2,1)S(1)}, u32[]{:S(2)}, u32[]{:S(2)}) collective-permute-start(bf16[512,768]{1,0:T(8,128)(2,1)S(1)} %fusion.13), channel_id=1, source_target_pairs={{0,8},{4,12},{8,0},{12,4},{1,9},{5,13},{9,1},{13,5},{2,10},{6,14},... | collective-permute-start | bytes 2359304 | tf_op jit(solution)/shard_map/ppermute | solution.py:423
  249.5 35.2 %copy-start.9 = (bf16[192,768]{1,0:T(8,128)(2,1)}, bf16[192,768]{1,0:T(8,128)(2,1)S(1)}, u32[]{:S(2)}) copy-start(bf16[192,768]{1,0:T(8,128)(2,1)S(1)} %add_convert_fusion.7) | copy-start | bytes 884740
  249.6 35.2 %collective-permute-start.51 = (bf16[192,768]{1,0:T(8,128)(2,1)S(1)}, bf16[192,768]{1,0:T(8,128)(2,1)S(1)}, u32[]{:S(2)}, u32[]{:S(2)}) collective-permute-start(bf16[192,768]{1,0:T(8,128)(2,1)S(1)} %add_convert_fusion.7), channel_id=1, source_target_pairs={{0,8},{4,12},{8,0},{12,4},{1,9},{5,13},{9,1},{13,5},{2,10},{6,14},... | collective-permute-start | bytes 884744 | tf_op jit(solution)/shard_map/ppermute | solution.py:423
  281.3 24.0 %collective-permute-start.28 = (bf16[512,768]{1,0:T(8,128)(2,1)}, bf16[512,768]{1,0:T(8,128)(2,1)}, u32[]{:S(2)}, u32[]{:S(2)}) collective-permute-start(bf16[512,768]{1,0:T(8,128)(2,1)} %get-tuple-element.143), channel_id=1, source_target_pairs={{0,8},{4,12},{8,0},{12,4},{1,9},{5,13},{9,1},{13,5},{2,10},{6,14},... | collective-permute-start | bytes 2359304 | tf_op jit(solution)/shard_map/ppermute | solution.py:423
  284.2 19.5 %collective-permute-start.57 = (f32[384,384]{1,0:T(8,128)}, f32[384,384]{1,0:T(8,128)}, u32[]{:S(2)}, u32[]{:S(2)}) collective-permute-start(f32[384,384]{1,0:T(8,128)} %convert_add_fusion.1), channel_id=1, source_target_pairs={{0,4},{4,0},{8,12},{12,8},{1,5},{5,1},{9,13},{13,9},{2,6},{6,2},{1... | collective-permute-start | bytes 1769480 | tf_op jit(solution)/shard_map/ppermute | solution.py:423
  285.7 22.3 %collective-permute-start.52 = (f32[192,768]{1,0:T(8,128)}, f32[192,768]{1,0:T(8,128)}, u32[]{:S(2)}, u32[]{:S(2)}) collective-permute-start(f32[192,768]{1,0:T(8,128)} %convert_add_fusion.2), channel_id=1, source_target_pairs={{0,4},{4,0},{8,12},{12,8},{1,5},{5,1},{9,13},{13,9},{2,6},{6,2},{1... | collective-permute-start | bytes 1769480 | tf_op jit(solution)/shard_map/ppermute | solution.py:423
  298.4 24.7 %collective-permute-start.27 = (bf16[512,768]{1,0:T(8,128)(2,1)}, bf16[512,768]{1,0:T(8,128)(2,1)S(1)}, u32[]{:S(2)}, u32[]{:S(2)}) collective-permute-start(bf16[512,768]{1,0:T(8,128)(2,1)} %get-tuple-element.143), channel_id=1, source_target_pairs={{0,4},{4,0},{8,12},{12,8},{1,5},{5,1},{9,13},{13,9},{2,6},{6,2},{1... | collective-permute-start | bytes 2359304 | tf_op jit(solution)/shard_map/ppermute | solution.py:423
  298.4 21.8 %collective-permute-start.19 = (bf16[512,768]{1,0:T(8,128)(2,1)S(1)}, bf16[512,768]{1,0:T(8,128)(2,1)}, u32[]{:S(2)}, u32[]{:S(2)}) collective-permute-start(bf16[512,768]{1,0:T(8,128)(2,1)S(1)} %get-tuple-element.219), channel_id=1, source_target_pairs={{0,1},{2,3},{4,5},{6,7},{8,9},{10,11},{12,13},{14,15},{16,17},{18,... | collective-permute-start | bytes 2359304 | tf_op jit(solution)/shard_map/ppermute | solution.py:449
  303.7 18.1 %collective-permute-start.22 = (bf16[512,768]{1,0:T(8,128)(2,1)S(1)}, bf16[512,768]{1,0:T(8,128)(2,1)}, u32[]{:S(2)}, u32[]{:S(2)}) collective-permute-start(bf16[512,768]{1,0:T(8,128)(2,1)S(1)} %get-tuple-element.219), channel_id=1, source_target_pairs={{3,2},{2,1},{7,6},{6,5},{11,10},{10,9},{15,14},{14,13},{19,18},{18... | collective-permute-start | bytes 2359304 | tf_op jit(solution)/shard_map/ppermute | solution.py:449
  305.3 17.8 %collective-permute-start.29 = (bf16[512,768]{1,0:T(8,128)(2,1)}, bf16[512,768]{1,0:T(8,128)(2,1)S(1)}, u32[]{:S(2)}, u32[]{:S(2)}) collective-permute-start(bf16[512,768]{1,0:T(8,128)(2,1)} %collective-permute-done.28), channel_id=1, source_target_pairs={{0,4},{4,0},{8,12},{12,8},{1,5},{5,1},{9,13},{13,9},{2,6},{6,2},{1... | collective-permute-start | bytes 2359304 | tf_op jit(solution)/shard_map/ppermute | solution.py:423
  320.2 106.7 %collective-permute-start.20 = (bf16[512,768]{1,0:T(8,128)(2,1)}, bf16[512,768]{1,0:T(8,128)(2,1)}, u32[]{:S(2)}, u32[]{:S(2)}) collective-permute-start(bf16[512,768]{1,0:T(8,128)(2,1)} %collective-permute-done.19), channel_id=1, source_target_pairs={{1,2},{5,6},{9,10},{13,14},{17,18},{21,22},{25,26},{29,30}} | collective-permute-start | bytes 2359304 | tf_op jit(solution)/shard_map/ppermute | solution.py:449
  321.8 106.7 %collective-permute-start.23 = (bf16[512,768]{1,0:T(8,128)(2,1)}, bf16[512,768]{1,0:T(8,128)(2,1)}, u32[]{:S(2)}, u32[]{:S(2)}) collective-permute-start(bf16[512,768]{1,0:T(8,128)(2,1)} %collective-permute-done.22), channel_id=1, source_target_pairs={{2,1},{1,0},{6,5},{5,4},{10,9},{9,8},{14,13},{13,12},{18,17},{17,1... | collective-permute-start | bytes 2359304 | tf_op jit(solution)/shard_map/ppermute | solution.py:449
  326.1 50.5 %copy-start.2 = (bf16[768,576]{1,0:T(8,128)(2,1)S(1)}, bf16[768,576]{1,0:T(8,128)(2,1)}, u32[]{:S(2)}) copy-start(bf16[768,576]{1,0:T(8,128)(2,1)} %all_gather.22.w_ref) | copy-start | bytes 2654212
  376.2 25.1 %collective-permute-start.43 = (bf16[192,384]{1,0:T(8,128)(2,1)}, bf16[192,384]{1,0:T(8,128)(2,1)}, u32[]{:S(2)}, u32[]{:S(2)}) collective-permute-start(bf16[192,384]{1,0:T(8,128)(2,1)} %dynamic-slice_convert_fusion.3), channel_id=1, source_target_pairs={{0,16},{16,0},{1,17},{17,1},{2,18},{18,2},{3,19},{19,3},{4,20},{20... | collective-permute-start | bytes 442376 | tf_op jit(solution)/shard_map/ppermute | solution.py:478
  387.7 32.0 %collective-permute-start.38 = (bf16[384,576]{0,1:T(8,128)(2,1)}, bf16[384,576]{0,1:T(8,128)(2,1)}, u32[]{:S(2)}, u32[]{:S(2)}) collective-permute-start(bf16[384,576]{0,1:T(8,128)(2,1)} %dynamic-slice_convert_fusion.2), channel_id=1, source_target_pairs={{0,16},{16,0},{1,17},{17,1},{2,18},{18,2},{3,19},{19,3},{4,20},{20... | collective-permute-start | bytes 1327112 | tf_op jit(solution)/shard_map/ppermute | solution.py:478
  393.1 24.4 %collective-permute-start.30 = (bf16[2,1,512,768]{3,2,1,0:T(8,128)(2,1)}, bf16[2,1,512,768]{3,2,1,0:T(8,128)(2,1)}, u32[]{:S(2)}, u32[]{:S(2)}) collective-permute-start(bf16[2,1,512,768]{3,2,1,0:T(8,128)(2,1)} %slice.264), channel_id=1, source_target_pairs={{0,4},{4,0},{8,12},{12,8},{1,5},{5,1},{9,13},{13,9},{2,6},{6,2},{1... | collective-permute-start | bytes 4718600 | tf_op jit(solution)/shard_map/ppermute | solution.py:423
  402.3 0.7 collective-permute-start.44
  403.1 26.8 %collective-permute-start.45 = (bf16[96,384]{1,0:T(8,128)(2,1)S(1)}, bf16[96,384]{1,0:T(8,128)(2,1)S(1)}, u32[]{:S(2)}, u32[]{:S(2)}) collective-permute-start(bf16[96,384]{1,0:T(8,128)(2,1)S(1)} %constant_dynamic-slice_fusion.3), channel_id=1, source_target_pairs={{0,4},{4,0},{8,12},{12,8},{1,5},{5,1},{9,13},{13,9},{2,6},{6,2},{1... | collective-permute-start | bytes 221192 | tf_op jit(solution)/shard_map/ppermute | solution.py:423
  419.7 20.5 %collective-permute-start.31 = (bf16[1,512,768]{2,1,0:T(8,128)(2,1)}, bf16[1,512,768]{2,1,0:T(8,128)(2,1)S(1)}, u32[]{:S(2)}, u32[]{:S(2)}) collective-permute-start(bf16[1,512,768]{2,1,0:T(8,128)(2,1)} %fusion.15), channel_id=1, source_target_pairs={{0,8},{4,12},{8,0},{12,4},{1,9},{5,13},{9,1},{13,5},{2,10},{6,14},... | collective-permute-start | bytes 2359304 | tf_op jit(solution)/shard_map/ppermute | solution.py:423
  421.6 8.5 %collective-permute-start.39 = (bf16[384,576]{0,1:T(8,128)(2,1)}, bf16[384,576]{0,1:T(8,128)(2,1)}, u32[]{:S(2)}, u32[]{:S(2)}) collective-permute-start(bf16[384,576]{0,1:T(8,128)(2,1)} %add_convert_fusion.5), channel_id=1, source_target_pairs={{0,0},{2,2},{3,3},{4,6},{6,4},{7,5},{8,9},{10,11},{11,10},{12,15},... | collective-permute-start | bytes 1327112 | tf_op jit(solution)/shard_map/ppermute | solution.py:445
  426.9 38.2 %collective-permute-start.21 = (bf16[512,768]{1,0:T(8,128)(2,1)}, bf16[512,768]{1,0:T(8,128)(2,1)}, u32[]{:S(2)}, u32[]{:S(2)}) collective-permute-start(bf16[512,768]{1,0:T(8,128)(2,1)} %collective-permute-done.20), channel_id=1, source_target_pairs={{2,3},{6,7},{10,11},{14,15},{18,19},{22,23},{26,27},{30,31}} | collective-permute-start | bytes 2359304 | tf_op jit(solution)/shard_map/ppermute | solution.py:449
  428.5 36.6 %collective-permute-start.24 = (bf16[512,768]{1,0:T(8,128)(2,1)}, bf16[512,768]{1,0:T(8,128)(2,1)}, u32[]{:S(2)}, u32[]{:S(2)}) collective-permute-start(bf16[512,768]{1,0:T(8,128)(2,1)} %collective-permute-done.23), channel_id=1, source_target_pairs={{1,0},{5,4},{9,8},{13,12},{17,16},{21,20},{25,24},{29,28}} | collective-permute-start | bytes 2359304 | tf_op jit(solution)/shard_map/ppermute | solution.py:449
  430.0 17.0 %collective-permute-start.46 = (bf16[96,384]{1,0:T(8,128)(2,1)S(1)}, bf16[96,384]{1,0:T(8,128)(2,1)S(1)}, u32[]{:S(2)}, u32[]{:S(2)}) collective-permute-start(bf16[96,384]{1,0:T(8,128)(2,1)S(1)} %add_convert_fusion.10), channel_id=1, source_target_pairs={{0,8},{4,12},{8,0},{12,4},{1,9},{5,13},{9,1},{13,5},{2,10},{6,14},... | collective-permute-start | bytes 221192 | tf_op jit(solution)/shard_map/ppermute | solution.py:423
  431.2 17.4 %collective-permute-start.40 = (bf16[192,576]{0,1:T(8,128)(2,1)S(1)}, bf16[192,576]{0,1:T(8,128)(2,1)S(1)}, u32[]{:S(2)}, u32[]{:S(2)}) collective-permute-start(bf16[192,576]{0,1:T(8,128)(2,1)S(1)} %constant_dynamic-slice_fusion.4), channel_id=1, source_target_pairs={{0,4},{4,0},{8,12},{12,8},{1,5},{5,1},{9,13},{13,9},{2,6},{6,2},{1... | collective-permute-start | bytes 663560 | tf_op jit(solution)/shard_map/ppermute | solution.py:423
  444.8 17.0 %collective-permute-start.32 = (bf16[512,768]{1,0:T(8,128)(2,1)S(1)}, bf16[512,768]{1,0:T(8,128)(2,1)}, u32[]{:S(2)}, u32[]{:S(2)}) collective-permute-start(bf16[512,768]{1,0:T(8,128)(2,1)S(1)} %fusion.16), channel_id=1, source_target_pairs={{0,1},{2,3},{4,5},{6,7},{8,9},{10,11},{12,13},{14,15},{16,17},{18,... | collective-permute-start | bytes 2359304 | tf_op jit(solution)/shard_map/ppermute | solution.py:449
  447.0 16.4 %collective-permute-start.35 = (bf16[512,768]{1,0:T(8,128)(2,1)S(1)}, bf16[512,768]{1,0:T(8,128)(2,1)}, u32[]{:S(2)}, u32[]{:S(2)}) collective-permute-start(bf16[512,768]{1,0:T(8,128)(2,1)S(1)} %fusion.16), channel_id=1, source_target_pairs={{3,2},{2,1},{7,6},{6,5},{11,10},{10,9},{15,14},{14,13},{19,18},{18... | collective-permute-start | bytes 2359304 | tf_op jit(solution)/shard_map/ppermute | solution.py:449
  448.6 1.4 collective-permute-start.47
  450.1 14.7 %collective-permute-start.41 = (bf16[192,576]{0,1:T(8,128)(2,1)S(1)}, bf16[192,576]{0,1:T(8,128)(2,1)S(1)}, u32[]{:S(2)}, u32[]{:S(2)}) collective-permute-start(bf16[192,576]{0,1:T(8,128)(2,1)S(1)} %add_convert_fusion.8), channel_id=1, source_target_pairs={{0,8},{4,12},{8,0},{12,4},{1,9},{5,13},{9,1},{13,5},{2,10},{6,14},... | collective-permute-start | bytes 663560 | tf_op jit(solution)/shard_map/ppermute | solution.py:423
  461.9 7.3 %collective-permute-start.33 = (bf16[512,768]{1,0:T(8,128)(2,1)}, bf16[512,768]{1,0:T(8,128)(2,1)}, u32[]{:S(2)}, u32[]{:S(2)}) collective-permute-start(bf16[512,768]{1,0:T(8,128)(2,1)} %collective-permute-done.32), channel_id=1, source_target_pairs={{1,2},{5,6},{9,10},{13,14},{17,18},{21,22},{25,26},{29,30}} | collective-permute-start | bytes 2359304 | tf_op jit(solution)/shard_map/ppermute | solution.py:449
  463.4 24.0 %collective-permute-start.36 = (bf16[512,768]{1,0:T(8,128)(2,1)}, bf16[512,768]{1,0:T(8,128)(2,1)}, u32[]{:S(2)}, u32[]{:S(2)}) collective-permute-start(bf16[512,768]{1,0:T(8,128)(2,1)} %collective-permute-done.35), channel_id=1, source_target_pairs={{2,1},{1,0},{6,5},{5,4},{10,9},{9,8},{14,13},{13,12},{18,17},{17,1... | collective-permute-start | bytes 2359304 | tf_op jit(solution)/shard_map/ppermute | solution.py:449
  465.0 3.9 collective-permute-start.42
  469.2 66.5 %collective-permute-start.34 = (bf16[512,768]{1,0:T(8,128)(2,1)}, bf16[512,768]{1,0:T(8,128)(2,1)}, u32[]{:S(2)}, u32[]{:S(2)}) collective-permute-start(bf16[512,768]{1,0:T(8,128)(2,1)} %collective-permute-done.33), channel_id=1, source_target_pairs={{2,3},{6,7},{10,11},{14,15},{18,19},{22,23},{26,27},{30,31}} | collective-permute-start | bytes 2359304 | tf_op jit(solution)/shard_map/ppermute | solution.py:449
  487.4 48.2 %collective-permute-start.37 = (bf16[512,768]{1,0:T(8,128)(2,1)}, bf16[512,768]{1,0:T(8,128)(2,1)}, u32[]{:S(2)}, u32[]{:S(2)}) collective-permute-start(bf16[512,768]{1,0:T(8,128)(2,1)} %collective-permute-done.36), channel_id=1, source_target_pairs={{1,0},{5,4},{9,8},{13,12},{17,16},{21,20},{25,24},{29,28}} | collective-permute-start | bytes 2359304 | tf_op jit(solution)/shard_map/ppermute | solution.py:449
  (65 other events, 401.1 us)
Sparse Core Ops, SparseCore 0:
  54.4 33.6 all-gather.5
  129.1 24.7 all-gather.7
